TPU v7x, 32 devices: a whole 2x2x4 slice. The times are simulated.
32 devices in a mesh: req: 4 (over z), ep: 8 (over y, x, core).
Axes of the slice: x: 2, y: 2, z: 4, core: 2. Of those that a mesh axis runs over, the one named last changes fastest.
Arguments:
- queries: bfloat16 [1024, 16, 192], P('ep'), may hold values from -260 to 260
- draft_latent: bfloat16 [1024, 576], P('ep'), may hold values from -5 to 5
- hidden_in: bfloat16 [1024, 2048], P('ep', 'req'), may hold values from -36 to 36
- cache_pool: bfloat16 [512, 128, 576], P(('req', 'ep')), may hold values from -5 to 5
- page_table: int32 [16, 32], P('ep'), may hold values from 0 to 15, as said below
- cache_len: int32 [16], P('ep'), may hold values from 1 to 3584
- parents: int32 [16, 64], P('ep'), may hold values from -1 to 62, as said below
- accept_leaf: int32 [16], P('ep'), may hold values from 0 to 63
- absorb_key: bfloat16 [16, 128, 512], replicated, may hold values from -0.5 to 0.5
- absorb_value: bfloat16 [16, 512, 128], replicated, may hold values from -0.25 to 0.25
- out_proj: bfloat16 [2048, 2048], P(None, 'req'), may hold values from -0.125 to 0.125
- norm_gain: float32 [2048], replicated, may hold values from 0.1 to 1.9
- router: bfloat16 [2048, 16], replicated, may hold values from -0.125 to 0.125
- expert_ids: int32 [1024, 6], P('ep'), may hold values from 0 to 15, all different within a row; in each aligned block of 128 rows (0 to 127, 128 to 255, ...) at most 96 rows name the same one
- expert_gate_up: bfloat16 [16, 2, 2048, 1408], P('ep', None, None, 'req'), may hold values from -0.125 to 0.125
- expert_down: bfloat16 [16, 1408, 2048], P('ep', 'req'), may hold values from -0.15625 to 0.15625
- shared_gate_up: bfloat16 [2, 2048, 1408], P(None, None, 'req'), may hold values from -0.125 to 0.125
- shared_down: bfloat16 [1408, 2048], P('req'), may hold values from -0.15625 to 0.15625
Outputs:
- layer_out: bfloat16 [1024, 2048], P('ep', 'req')
- new_pages: bfloat16 [16, 4, 128, 576], P('ep', 'req')
Inputs may be any that keep to these rules, and one draw needn't show every extreme that they name: `page_table`: for the 2 requests of one ep index, the pages j with one value of j mod 4 name distinct slots. parents[r, i] < i, and it is -1 exactly at i = 0. `expert_ids`: in each aligned block of 128 rows no expert is named by more than 96 rows.
All inputs are finite; a program needn't handle non-finite values.
Results may differ from a plain program's by a relative error of at most 0.011.
Values may be sent and summed in bfloat16 or wider, within the bound.
A program may use at most 128 MiB of HBM per device.

v0:
```python
import math

import jax
import jax.numpy as jnp
from jax import lax
from jax.sharding import PartitionSpec as P

NEGATIVE = -1e30


def joined_2(array, axis, combine):
    everything = jax.tree.map(lambda part: lax.all_gather(part, axis), array)
    leading = jax.tree.map(lambda part: part[0], everything)

    def turn(k, so_far):
        return combine(so_far, jax.tree.map(lambda part: part[k], everything))

    return lax.fori_loop(1, lax.axis_size(axis), turn, leading)


def ancestors(parents):
    draft_count = parents.shape[-1]
    draft_index = jnp.arange(draft_count, dtype=jnp.int32)
    ancestry = (parents[:, :, None] == draft_index[None, None, :]).astype(jnp.float32)
    ancestry = ancestry + jnp.eye(draft_count, dtype=jnp.float32)[None]
    for doubling in range(max(1, (draft_count - 1).bit_length())):
        ancestry = jnp.minimum(
            jnp.einsum("rij,rjk->rik", ancestry, ancestry, precision=lax.Precision.HIGHEST), 1.0
        )
    return ancestry


def combine_states(left_state, right_state):
    joined = jnp.maximum(left_state[0], right_state[0])
    left_factor = jnp.exp(left_state[0] - joined)
    right_factor = jnp.exp(right_state[0] - joined)
    summed = left_state[1] * left_factor + right_state[1] * right_factor
    mixed = left_state[2] * left_factor[..., None] + right_state[2] * right_factor[..., None]
    return (joined, summed, mixed)


def per_device(
    queries,
    draft_latent,
    hidden_in,
    cache_pool,
    page_table,
    cache_len,
    parents,
    accept_leaf,
    absorb_key,
    absorb_value,
    out_proj,
    norm_gain,
    router,
    expert_ids,
    expert_gate_up,
    expert_down,
    shared_gate_up,
    shared_down,
):
    highest = lax.Precision.HIGHEST
    req_count = lax.axis_size("req")
    req_index = lax.axis_index("req")
    ep_count = lax.axis_size("ep")
    request_count, draft_count = parents.shape
    token_count = request_count * draft_count
    head_count = queries.shape[1]
    nope_width = absorb_key.shape[1]
    latent_width = absorb_key.shape[2]
    page_size = cache_pool.shape[1]
    key_width = cache_pool.shape[2]
    page_count = page_table.shape[1]
    score_scale = 1.0 / math.sqrt(queries.shape[2])
    ancestry = ancestors(parents)
    depths = jnp.sum(ancestry, axis=2) - 1.0
    local_pages = page_count // req_count
    page_cols = req_index + req_count * jnp.arange(local_pages, dtype=jnp.int32)
    slot_rows = jnp.take(page_table, page_cols, axis=1)
    cached = cache_pool[slot_rows].reshape(request_count, local_pages * page_size, key_width)
    positions = (
        page_cols[:, None] * page_size + jnp.arange(page_size, dtype=jnp.int32)[None, :]
    ).reshape(-1)
    cache_ok = positions[None, :] < cache_len[:, None]
    draft_share = draft_count // req_count
    draft_cols = req_index * draft_share + jnp.arange(draft_share, dtype=jnp.int32)
    own_latent = draft_latent.reshape(request_count, draft_count, key_width)
    draft_keys = jnp.take(own_latent, draft_cols, axis=1)
    tree_ok = jnp.take(ancestry, draft_cols, axis=2) > 0.5
    absorbed = jnp.einsum(
        "thd,hdl->thl", queries[:, :, :nope_width], absorb_key, preferred_element_type=jnp.float32
    ).astype(jnp.bfloat16)
    query_full = jnp.concatenate([absorbed, queries[:, :, nope_width:]], axis=2)
    query_full = query_full.reshape(request_count, draft_count, head_count, key_width)
    score_cache = (
        jnp.einsum("rthk,rsk->rths", query_full, cached, preferred_element_type=jnp.float32)
        * score_scale
    )
    score_cache = jnp.where(cache_ok[:, None, None, :], score_cache, NEGATIVE)
    score_draft = (
        jnp.einsum("rthk,rsk->rths", query_full, draft_keys, preferred_element_type=jnp.float32)
        * score_scale
    )
    score_draft = jnp.where(tree_ok[:, :, None, :], score_draft, NEGATIVE)
    highest_score = jnp.maximum(jnp.max(score_cache, axis=3), jnp.max(score_draft, axis=3))
    weight_cache = jnp.where(
        cache_ok[:, None, None, :], jnp.exp(score_cache - highest_score[..., None]), 0.0
    )
    weight_draft = jnp.where(
        tree_ok[:, :, None, :], jnp.exp(score_draft - highest_score[..., None]), 0.0
    )
    totals = jnp.sum(weight_cache, axis=3) + jnp.sum(weight_draft, axis=3)
    mixed_latent = jnp.einsum(
        "rths,rsl->rthl",
        weight_cache.astype(jnp.bfloat16),
        cached[:, :, :latent_width],
        preferred_element_type=jnp.float32,
    )
    mixed_latent = mixed_latent + jnp.einsum(
        "rths,rsl->rthl",
        weight_draft.astype(jnp.bfloat16),
        draft_keys[:, :, :latent_width],
        preferred_element_type=jnp.float32,
    )
    value_weight = absorb_value.astype(jnp.float32)
    merged = joined_2((highest_score, totals, mixed_latent), "req", combine_states)
    head_out = jnp.einsum(
        "rthl,hlv->rthv", merged[2] / merged[1][..., None], value_weight, precision=highest
    )
    head_rows = head_out.astype(jnp.bfloat16).reshape(token_count, -1)
    attention = jnp.dot(head_rows, out_proj, preferred_element_type=jnp.float32)
    resid_cols = (hidden_in.astype(jnp.float32) + attention).astype(jnp.bfloat16)
    resid = lax.all_gather(resid_cols, "req", axis=1, tiled=True)
    resid_wide = resid.astype(jnp.float32)
    normed = resid_wide * lax.rsqrt(
        jnp.mean(resid_wide * resid_wide, axis=1, keepdims=True) + 1e-06
    )
    normed = (normed * norm_gain[None, :]).astype(jnp.bfloat16)
    logits = jnp.dot(normed, router, preferred_element_type=jnp.float32)
    lifted = jax.nn.sigmoid(jnp.take_along_axis(logits, expert_ids, axis=1))
    gates = lifted / jnp.sum(lifted, axis=1, keepdims=True)
    shared_gate = jnp.dot(normed, shared_gate_up[0], preferred_element_type=jnp.float32)
    shared_lift = jnp.dot(normed, shared_gate_up[1], preferred_element_type=jnp.float32)
    shared_hidden = (jax.nn.silu(shared_gate) * shared_lift).astype(jnp.bfloat16)
    shared_part = jnp.dot(shared_hidden, shared_down, preferred_element_type=jnp.float32)
    route_width = expert_ids.shape[1]
    local_experts = expert_gate_up.shape[0]
    expert_total = local_experts * ep_count
    capacity = (2 * token_count * route_width + expert_total - 1) // expert_total
    pair_experts = expert_ids.reshape(-1)
    marks = (pair_experts[:, None] == jnp.arange(expert_total, dtype=jnp.int32)[None, :]).astype(
        jnp.int32
    )
    slot_of = jnp.sum(jnp.cumsum(marks, axis=0) * marks, axis=1) - 1
    placement = pair_experts * capacity + slot_of
    pair_token = jnp.arange(token_count * route_width, dtype=jnp.int32) // route_width
    source = (
        jnp.full((expert_total * capacity,), token_count, dtype=jnp.int32)
        .at[placement]
        .set(pair_token)
    )
    padded = jnp.concatenate([normed, jnp.zeros((1, normed.shape[1]), jnp.bfloat16)], axis=0)
    gate_weight = expert_gate_up[:, 0]
    lift_weight = expert_gate_up[:, 1]
    outgoing = padded[source].reshape(ep_count, local_experts, capacity, -1)
    incoming = lax.all_to_all(outgoing, "ep", split_axis=0, concat_axis=0, tiled=True)
    gate_value = jnp.einsum(
        "pecd,edf->pecf", incoming, gate_weight, preferred_element_type=jnp.float32
    )
    lift_value = jnp.einsum(
        "pecd,edf->pecf", incoming, lift_weight, preferred_element_type=jnp.float32
    )
    hidden_rows = (jax.nn.silu(gate_value) * lift_value).astype(jnp.bfloat16)
    result = jnp.einsum(
        "pecf,efd->pecd", hidden_rows, expert_down, preferred_element_type=jnp.float32
    )
    returned = lax.all_to_all(
        result.astype(jnp.bfloat16), "ep", split_axis=0, concat_axis=0, tiled=True
    ).astype(result.dtype)
    picked = returned.reshape(expert_total * capacity, -1)[placement].reshape(
        token_count, route_width, -1
    )
    routed = jnp.sum(gates[:, :, None] * picked, axis=1)
    term = shared_part + routed
    summed = lax.psum_scatter(
        term.astype(jnp.bfloat16), "req", scatter_dimension=1, tiled=True
    ).astype(jnp.float32)
    layer_out = (resid_cols.astype(jnp.float32) + summed).astype(jnp.bfloat16)
    starts = cache_len // page_size
    page_now = starts + jnp.mod(req_index - starts, req_count)
    slot_now = jnp.take_along_axis(page_table, page_now[:, None], axis=1)[:, 0]
    old_page = cache_pool[slot_now]
    offsets = (
        page_now[:, None] * page_size
        + jnp.arange(page_size, dtype=jnp.int32)[None, :]
        - cache_len[:, None]
    ).astype(jnp.float32)
    accepted = jnp.take_along_axis(ancestry, accept_leaf[:, None, None], axis=1)[:, 0, :]
    select = accepted[:, None, :] * (depths[:, None, :] == offsets[:, :, None]).astype(jnp.float32)
    written = jnp.einsum(
        "rod,rdk->rok", select.astype(jnp.bfloat16), own_latent, preferred_element_type=jnp.float32
    )
    touched = jnp.sum(select, axis=2) > 0.5
    fresh = jnp.where(touched[..., None], written, old_page.astype(jnp.float32)).astype(
        jnp.bfloat16
    )
    return (layer_out, fresh[:, None])


def solution(mesh):
    in_specs = (
        P("ep", None, None),
        P("ep", None),
        P("ep", "req"),
        P(("req", "ep"), None, None),
        P("ep", None),
        P("ep"),
        P("ep", None),
        P("ep"),
        P(),
        P(),
        P(None, "req"),
        P(),
        P(),
        P("ep", None),
        P("ep", None, None, "req"),
        P("ep", "req", None),
        P(None, None, "req"),
        P("req", None),
    )
    out_specs = (P("ep", "req"), P("ep", "req", None, None))
    return jax.shard_map(
        per_device, mesh=mesh, in_specs=in_specs, out_specs=out_specs, check_vma=False
    )
```

profile of v0, /device:TPU:0, one launch (start us, length us, event | category | flops | bytes accessed | tf_op | source)
XLA Modules:
  0.0 661.0 jit_solution(8534095624826168476)
XLA Ops:
  11.6 4.9 copy.124
  17.4 4.0 gather_fusion.1
  21.4 4.4 copy.127
  27.5 6.6 fusion.86
  38.8 9.3 %fusion.3 = (f32[2,64,16]{2,1,0:T(8,128)S(1)}, f32[2,64,16,1024]{3,2,1,0:T(8,128)}) fusion(pred[2,1024]{1,0:T(4,128)(4,1)S(1)} %broadcast_compare_fusion, bf16[2,64,16,576]{3,2,1,0:T(8,128)(2,1)} %bitcast.199, bf16[2,1024,576,1]{2,1,3,0:T(8,128)(2,1)} %bitcast.200), kind=kOutput, calls=%fused_computation.22 | convolution fusion | flops 2422208512 | bytes 13117440 | tf_op jit(solution)/shard_map/rthk,rsk->rths/dot_general | solution.py:96
  50.9 5.6 fusion.10
  60.2 15.2 %all-gather = f32[8,64,16]{1,2,0:T(8,128)S(1)} all-gather(f32[2,64,16]{1,2,0:T(8,128)S(1)} %copy-done.13), channel_id=2, replica_groups=mesh['req'=4,'ep'=8] {'req'}, dimensions={0}, use_global_device_ids=true | all-gather | bytes 40960 | tf_op jit(solution)/shard_map/all_gather | solution.py:12
  75.4 5.4 fusion.5
  80.9 22.1 %all-gather.1 = f32[8,64,16]{1,2,0:T(8,128)S(1)} all-gather(f32[2,64,16]{1,2,0:T(8,128)S(1)} %copy.141), channel_id=3, replica_groups=mesh['req'=4,'ep'=8] {'req'}, dimensions={0}, use_global_device_ids=true | all-gather | bytes 40960 | tf_op jit(solution)/shard_map/all_gather | solution.py:12
  105.4 3.4 scatter_custom_fusion
  108.8 240.9 %all-gather.5.cloned.1.call-done = f32[8,64,16,512]{3,2,1,0:T(8,128)} async-done(((f32[2,64,16,512]{3,2,1,0:T(8,128)}), f32[8,64,16,512]{3,2,1,0:T(8,128)}) %all-gather.5.cloned.1.call-update) | async-done | bytes 16777232 | tf_op jit(solution)/shard_map/all_gather | solution.py:12
  349.7 5.0 slice.79
  354.7 16.0 %while.19 = (s32[]{:T(128)}, f32[2,64,16]{1,2,0:T(8,128)S(1)}, f32[2,64,16]{1,2,0:T(8,128)S(1)}, f32[2,64,16,512]{3,2,1,0:T(8,128)}, f32[4,2,64,16]{2,3,1,0:T(8,...) while((s32[]{:T(128)}, f32[2,64,16]{1,2,0:T(8,128)S(1)}, ...), condition=%wide.region_5.6_spmd, body=%wide.region_4.5_spmd.sunk | while | flops 3158021 | bytes 12697751 | solution.py:18
  354.9 5.1 fusion.145
  360.2 5.1 fusion.145
  365.6 5.1 fusion.145
  373.6 4.4 fusion.49
  378.9 16.2 %all_gather.21 = bf16[128,2048]{1,0:T(8,128)(2,1)S(1)} all-gather(bf16[128,512]{1,0:T(8,128)(2,1)S(1)} %fusion.57), channel_id=1, replica_groups=mesh['req'=4,'ep'=8] {'req'}, dimensions={1}, use_global_device_ids=true | all-gather | bytes 655360 | tf_op jit(solution)/shard_map/all_gather | solution.py:133
  396.4 7.1 %gather_fusion.4 = bf16[1536,2048]{1,0:T(8,128)(2,1)} fusion(bf16[129,2048]{1,0:T(8,128)(2,1)S(1)} %concatenate.7, s32[2048]{0:T(1024)S(1)} %pad_clamp_fusion), kind=kCustom, calls=%fused_computation.4 | custom fusion | bytes 12589056 | tf_op jit(solution)/shard_map/gather | solution.py:165
  403.5 86.1 %all_to_all.10 = bf16[8,2,96,2048]{3,2,1,0:T(8,128)(2,1)S(1)} all-to-all(bf16[8,2,96,2048]{3,2,1,0:T(8,128)(2,1)} %bitcast.197), channel_id=1, replica_groups=mesh['req'=4,'ep'=8] {'ep'}, dimensions={0} | all-to-all | bytes 12582912 | tf_op jit(solution)/shard_map/all_to_all | solution.py:166
  492.2 6.7 %fusion.8 = f32[2,8,96,352]{3,2,1,0:T(8,128)} fusion(bf16[8,2,96,2048]{3,2,1,0:T(8,128)(2,1)S(1)} %all_to_all.10, bf16[2,2,2048,352]{2,3,1,0:T(8,128)(2,1)} %param.34), kind=kOutput, calls=%fused_computation.29 | convolution fusion | flops 2214592512 | bytes 11337728 | tf_op jit(solution)/shard_map/pecd,edf->pecf/dot_general | solution.py:167
  498.9 11.2 %convert_bitcast_fusion = bf16[8,2,96,2048]{3,2,0,1:T(8,128)(2,1)} fusion(bf16[2,352,2048]{2,1,0:T(8,128)(2,1)S(1)} %copy-done, f32[2,8,96,352]{3,2,1,0:T(8,128)} %fusion.8, bf16[2,2,2048,352]{2,3,1,0:T(8,128)(2,1)} %param.34, bf16[8,2,96,2048]{3,2,1,0:T(8,128)(2,1)} %copy-done.5), kind=kOutput, calls=%fused_computation.24 | convolution fusion | flops 4435574784 | bytes 20709376 | tf_op jit(solution)/shard_map/pecf,efd->pecd/dot_general | solution.py:174
  510.1 6.6 copy.157
  516.6 4.9 all-to-all-start.1
  527.6 5.1 gather_fusion.7
  535.7 57.5 %all-to-all-done.1 = bf16[8,2,96,2048]{3,2,1,0:T(8,128)(2,1)} async-done(((bf16[8,2,96,2048]{3,2,1,0:T(8,128)(2,1)}), bf16[8,2,96,2048]{3,2,1,0:T(8,128)(2,1)}, u32[]{:S(2)}, u32[]{:S(2)}) %all-to-all-start.1) | async-done | bytes 6291488 | tf_op jit(solution)/shard_map/all_to_all | solution.py:177
  593.2 8.9 %bitcast_convert_fusion = f32[1536,2048]{1,0:T(8,128)} fusion(bf16[8,2,96,2048]{3,2,1,0:T(8,128)(2,1)} %all-to-all-done.1), kind=kLoop, calls=%fused_computation.23 | loop fusion | flops 3145728 | bytes 18874368 | tf_op jit(solution)/shard_map/reshape | solution.py:180
  602.0 11.8 %gather_fusion.5 = f32[768,2048]{1,0:T(8,128)} fusion(f32[1536,2048]{1,0:T(8,128)} %bitcast_convert_fusion, s32[1024]{0:T(1024)S(1)} %pad_clamp_fusion.2), kind=kCustom, calls=%fused_computation.5 | custom fusion | bytes 12585984 | tf_op jit(solution)/shard_map/gather | solution.py:180
  613.8 7.8 %reshape.374 = f32[128,6,2048]{2,1,0:T(8,128)} reshape(f32[768,2048]{1,0:T(8,128)} %gather_fusion.5) | data formatting | bytes 12582912 | tf_op jit(solution)/shard_map/reshape | solution.py:180
  621.7 7.8 %multiply_reduce_fusion = f32[128,2048]{1,0:T(8,128)} fusion(f32[128,6,2048]{2,1,0:T(8,128)} %reshape.374, f32[128,6]{1,0:T(8,128)S(1)} %copy.148), kind=kLoop, calls=%fused_computation.19 | loop fusion | flops 2883584 | bytes 7343104 | tf_op jit(solution)/shard_map/reduce_sum | solution.py:183
  629.5 4.5 fusion.24
  636.3 16.0 %reduce-scatter.2.cloned.1.call-done = bf16[128,512]{1,0:T(8,128)(2,1)} async-done(((bf16[128,2048]{1,0:T(8,128)(2,1)}), bf16[128,512]{1,0:T(8,128)(2,1)}) %reduce-scatter.2.cloned.1.call-update) | async-done | bytes 131088 | tf_op jit(solution)/shard_map/reduce_scatter | solution.py:185
  (168 shorter events, 41.5 us)
Async XLA Ops:
  7.2 491.7 %copy-start = (bf16[2,352,2048]{2,1,0:T(8,128)(2,1)S(1)}, bf16[2,352,2048]{2,1,0:T(8,128)(2,1)}, u32[]{:S(2)}) copy-start(bf16[2,352,2048]{2,1,0:T(8,128)(2,1)} %param.35) | copy-start | bytes 8650756
  7.2 2.8 slice-start
  7.2 342.6 %all-gather.5.cloned.1.call-start = ((), (), s32[]{:S(2)}) async-start(), calls=%async_computation.4 | async-start | bytes 20971520 | tf_op jit(solution)/shard_map/all_gather | solution.py:12
  10.0 6.5 copy-start.2
  17.4 8.4 %copy-start.11 = (bf16[128,576]{0,1:T(8,128)(2,1)S(1)}, bf16[128,576]{0,1:T(8,128)(2,1)}, u32[]{:S(2)}) copy-start(bf16[128,576]{0,1:T(8,128)(2,1)} %param.21) | copy-start | bytes 442372
  21.4 14.4 %copy-start.23 = (s32[2,64]{1,0:T(2,128)S(1)}, s32[2,64]{1,0:T(2,128)}, u32[]{:S(2)}) copy-start(s32[2,64]{1,0:T(2,128)} %param.26) | copy-start | bytes 1540
  25.8 12.9 %copy-start.20 = (s32[2]{0:T(128)S(1)}, s32[2]{0:T(128)}, u32[]{:S(2)}) copy-start(s32[2]{0:T(128)} %param.25) | copy-start | bytes 28
  25.9 1.5 copy-start.8
  48.2 1.3 copy-start.12
  50.8 5.6 copy-start.14
  59.1 0.7 copy-start.16
  59.1 1.1 copy-start.13
  59.1 16.2 %copy-start.18 = (f32[2,64,16]{1,2,0:T(8,128)S(1)}, f32[2,64,16]{1,2,0:T(8,128)}, u32[]{:S(2)}) copy-start(f32[2,64,16]{1,2,0:T(8,128)} %get-tuple-element.210) | copy-start | bytes 24580
  370.8 2.9 copy-start.6
  373.6 4.8 copy-start.7
  373.6 4.8 copy-start.15
  378.1 17.3 %copy-start.19 = (f32[2048]{0:T(1024)S(1)}, f32[2048]{0:T(1024)}, u32[]{:S(2)}) copy-start(f32[2048]{0:T(1024)} %param.31) | copy-start | bytes 24580
  378.9 16.7 %copy-start.9 = (bf16[128,512]{1,0:T(8,128)(2,1)}, bf16[128,512]{1,0:T(8,128)(2,1)S(1)}, u32[]{:S(2)}) copy-start(bf16[128,512]{1,0:T(8,128)(2,1)S(1)} %fusion.57) | copy-start | bytes 393220
  395.6 0.8 copy-start.3
  489.6 2.7 copy-start.5
  516.6 5.3 copy-start.24
  516.6 10.7 %copy-start.4 = (bf16[128,2048]{1,0:T(8,128)(2,1)S(1)}, bf16[128,2048]{1,0:T(8,128)(2,1)}, u32[]{:S(2)}) copy-start(bf16[128,2048]{1,0:T(8,128)(2,1)} %copy-done.3) | copy-start | bytes 1572868
  516.6 10.7 %copy-start.17 = (bf16[2048,16]{0,1:T(8,128)(2,1)S(1)}, bf16[2048,16]{0,1:T(8,128)(2,1)}, u32[]{:S(2)}) copy-start(bf16[2048,16]{0,1:T(8,128)(2,1)} %param.32) | copy-start | bytes 196612
  516.6 76.5 %all-to-all-start.1 = ((bf16[8,2,96,2048]{3,2,1,0:T(8,128)(2,1)}), bf16[8,2,96,2048]{3,2,1,0:T(8,128)(2,1)}, u32[]{:S(2)}, u32[]{:S(2)}) async-start(bf16[8,2,96,2048]{3,2,1,0:T(8,128)(2,1)} %copy.157), calls=%async_computation.1 | async-start | bytes 12582912 | tf_op jit(solution)/shard_map/all_to_all | solution.py:177
  521.6 130.8 %reduce-scatter.2.cloned.1.call-start = ((), (), s32[]{:S(2)}) async-start(), calls=%async_computation.3 | async-start | bytes 655360 | tf_op jit(solution)/shard_map/reduce_scatter | solution.py:185
  621.7 32.3 %copy-start.1 = (bf16[2,352,2048]{2,1,0:T(8,128)(2,1)S(1)}, bf16[2,352,2048]{2,1,0:T(8,128)(2,1)}, u32[]{:S(2)}) copy-start(bf16[2,352,2048]{2,1,0:T(8,128)(2,1)} %param.35) | copy-start | bytes 8650756
  629.4 4.5 copy-start.25
  629.4 4.6 copy-start.21
  629.5 4.6 copy-start.22
  629.5 22.9 %copy-start.10 = (bf16[128,512]{1,0:T(8,128)(2,1)S(1)}, bf16[128,512]{1,0:T(8,128)(2,1)}, u32[]{:S(2)}) copy-start(bf16[128,512]{1,0:T(8,128)(2,1)} %copy-done.9) | copy-start | bytes 393220
Sparse Core Ops, SparseCore 0:
  59.2 290.4 all-gather.4
  634.1 18.1 reduce-scatter.1
where the time goes:
time: 665 us; the launch traced here: 661 us
  waiting for transfers between devices  314 us (47%)
  blocking collectives  140 us (21%)
  local copies, waits for them, and re-layouts  77.4 us (12%)
  matrix products  60.8 us (9%)
  other arithmetic  49 us (7%)
  between operations  14.8 us (2%)
    all_gather x1, waiting for transfers between devices, joined_2(): everything = jax.tree.map(lambda part: lax.all_gather(part, axis), array)  241 us
    all_to_all x1, blocking collectives, per_device(): lax.all_to_all(outgoing, 'ep', split_axis=0, concat_axis=0, tiled=True)  86.1 us
    all_to_all x1, waiting for transfers between devices, per_device(): lax.all_to_all(result.astype(jnp.bfloat16), 'ep', split_axis=0, concat_ax...  57.5 us
    all_gather x2, blocking collectives, joined_2(): everything = jax.tree.map(lambda part: lax.all_gather(part, axis), array)  37.3 us
    all_gather x1, blocking collectives, per_device(): resid = lax.all_gather(resid_cols, 'req', axis=1, tiled=True)  16.2 us
    reduce_scatter x1, waiting for transfers between devices, per_device(): lax.psum_scatter(term.astype(jnp.bfloat16), 'req', scatter_dimension=1, t...  16 us
    add x3, other arithmetic, combine_states(): left_state[2] * left_factor[..., None]  15.4 us
  transfers between devices with their start and end apart: 3, of which 3 were waited for; matrix products, arithmetic and copies ran while one was open for 4% of the time, Pallas kernels for 0%

commit v1 on v0

--- a/solution.py
+++ b/solution.py
@@ -6,16 +6,6 @@
 from jax.sharding import PartitionSpec as P
 
 NEGATIVE = -1e30
-
-
-def joined_2(array, axis, combine):
-    everything = jax.tree.map(lambda part: lax.all_gather(part, axis), array)
-    leading = jax.tree.map(lambda part: part[0], everything)
-
-    def turn(k, so_far):
-        return combine(so_far, jax.tree.map(lambda part: part[k], everything))
-
-    return lax.fori_loop(1, lax.axis_size(axis), turn, leading)
 
 
 def ancestors(parents):
@@ -28,15 +18,6 @@
             jnp.einsum("rij,rjk->rik", ancestry, ancestry, precision=lax.Precision.HIGHEST), 1.0
         )
     return ancestry
-
-
-def combine_states(left_state, right_state):
-    joined = jnp.maximum(left_state[0], right_state[0])
-    left_factor = jnp.exp(left_state[0] - joined)
-    right_factor = jnp.exp(right_state[0] - joined)
-    summed = left_state[1] * left_factor + right_state[1] * right_factor
-    mixed = left_state[2] * left_factor[..., None] + right_state[2] * right_factor[..., None]
-    return (joined, summed, mixed)
 
 
 def per_device(
@@ -59,7 +40,6 @@
     shared_gate_up,
     shared_down,
 ):
-    highest = lax.Precision.HIGHEST
     req_count = lax.axis_size("req")
     req_index = lax.axis_index("req")
     ep_count = lax.axis_size("ep")
@@ -122,11 +102,17 @@
         draft_keys[:, :, :latent_width],
         preferred_element_type=jnp.float32,
     )
-    value_weight = absorb_value.astype(jnp.float32)
-    merged = joined_2((highest_score, totals, mixed_latent), "req", combine_states)
-    head_out = jnp.einsum(
-        "rthl,hlv->rthv", merged[2] / merged[1][..., None], value_weight, precision=highest
-    )
+    projected = jnp.einsum(
+        "rthl,hlv->rthv",
+        mixed_latent.astype(jnp.bfloat16),
+        absorb_value,
+        preferred_element_type=jnp.float32,
+    ).astype(jnp.bfloat16)
+    stats = lax.all_gather(jnp.stack([highest_score, totals]), "req")
+    parts = lax.all_gather(projected, "req").astype(jnp.float32)
+    factors = jnp.exp(stats[:, 0] - jnp.max(stats[:, 0], axis=0)[None])
+    factors = factors / jnp.sum(factors * stats[:, 1], axis=0)[None]
+    head_out = jnp.sum(parts * factors[..., None], axis=0)
     head_rows = head_out.astype(jnp.bfloat16).reshape(token_count, -1)
     attention = jnp.dot(head_rows, out_proj, preferred_element_type=jnp.float32)
     resid_cols = (hidden_in.astype(jnp.float32) + attention).astype(jnp.bfloat16)
@@ -136,54 +122,39 @@
         jnp.mean(resid_wide * resid_wide, axis=1, keepdims=True) + 1e-06
     )
     normed = (normed * norm_gain[None, :]).astype(jnp.bfloat16)
+    everyone = lax.all_gather(normed, "ep", axis=0, tiled=True)
+    local_experts = expert_gate_up.shape[0]
+    expert_total = local_experts * ep_count
+    named = jnp.any(
+        expert_ids[:, :, None] == jnp.arange(expert_total, dtype=jnp.int32)[None, None, :], axis=1
+    ).astype(jnp.float32)
     logits = jnp.dot(normed, router, preferred_element_type=jnp.float32)
-    lifted = jax.nn.sigmoid(jnp.take_along_axis(logits, expert_ids, axis=1))
+    lifted = jax.nn.sigmoid(logits) * named
     gates = lifted / jnp.sum(lifted, axis=1, keepdims=True)
+    gates_all = lax.all_gather(gates, "ep", axis=0, tiled=True)
+    own_gates = lax.dynamic_slice_in_dim(
+        gates_all, lax.axis_index("ep") * local_experts, local_experts, axis=1
+    )
     shared_gate = jnp.dot(normed, shared_gate_up[0], preferred_element_type=jnp.float32)
     shared_lift = jnp.dot(normed, shared_gate_up[1], preferred_element_type=jnp.float32)
     shared_hidden = (jax.nn.silu(shared_gate) * shared_lift).astype(jnp.bfloat16)
     shared_part = jnp.dot(shared_hidden, shared_down, preferred_element_type=jnp.float32)
-    route_width = expert_ids.shape[1]
-    local_experts = expert_gate_up.shape[0]
-    expert_total = local_experts * ep_count
-    capacity = (2 * token_count * route_width + expert_total - 1) // expert_total
-    pair_experts = expert_ids.reshape(-1)
-    marks = (pair_experts[:, None] == jnp.arange(expert_total, dtype=jnp.int32)[None, :]).astype(
-        jnp.int32
-    )
-    slot_of = jnp.sum(jnp.cumsum(marks, axis=0) * marks, axis=1) - 1
-    placement = pair_experts * capacity + slot_of
-    pair_token = jnp.arange(token_count * route_width, dtype=jnp.int32) // route_width
-    source = (
-        jnp.full((expert_total * capacity,), token_count, dtype=jnp.int32)
-        .at[placement]
-        .set(pair_token)
-    )
-    padded = jnp.concatenate([normed, jnp.zeros((1, normed.shape[1]), jnp.bfloat16)], axis=0)
-    gate_weight = expert_gate_up[:, 0]
-    lift_weight = expert_gate_up[:, 1]
-    outgoing = padded[source].reshape(ep_count, local_experts, capacity, -1)
-    incoming = lax.all_to_all(outgoing, "ep", split_axis=0, concat_axis=0, tiled=True)
-    gate_value = jnp.einsum(
-        "pecd,edf->pecf", incoming, gate_weight, preferred_element_type=jnp.float32
-    )
-    lift_value = jnp.einsum(
-        "pecd,edf->pecf", incoming, lift_weight, preferred_element_type=jnp.float32
-    )
-    hidden_rows = (jax.nn.silu(gate_value) * lift_value).astype(jnp.bfloat16)
-    result = jnp.einsum(
-        "pecf,efd->pecd", hidden_rows, expert_down, preferred_element_type=jnp.float32
-    )
-    returned = lax.all_to_all(
-        result.astype(jnp.bfloat16), "ep", split_axis=0, concat_axis=0, tiled=True
-    ).astype(result.dtype)
-    picked = returned.reshape(expert_total * capacity, -1)[placement].reshape(
-        token_count, route_width, -1
-    )
-    routed = jnp.sum(gates[:, :, None] * picked, axis=1)
-    term = shared_part + routed
+    term = 0.0
+    for e in range(local_experts):
+        gate_value = jnp.dot(
+            everyone, expert_gate_up[e, 0], preferred_element_type=jnp.float32
+        )
+        lift_value = jnp.dot(
+            everyone, expert_gate_up[e, 1], preferred_element_type=jnp.float32
+        )
+        hidden_rows = (jax.nn.silu(gate_value) * lift_value).astype(jnp.bfloat16)
+        result = jnp.dot(hidden_rows, expert_down[e], preferred_element_type=jnp.float32)
+        term = term + own_gates[:, e : e + 1] * result
+    routed = lax.psum_scatter(
+        term.astype(jnp.bfloat16), "ep", scatter_dimension=0, tiled=True
+    ).astype(jnp.float32)
     summed = lax.psum_scatter(
-        term.astype(jnp.bfloat16), "req", scatter_dimension=1, tiled=True
+        (shared_part + routed).astype(jnp.bfloat16), "req", scatter_dimension=1, tiled=True
     ).astype(jnp.float32)
     layer_out = (resid_cols.astype(jnp.float32) + summed).astype(jnp.bfloat16)
     starts = cache_len // page_size

time: 665 us -> 302 us (0.45)
  waiting for transfers between devices: 314 us -> 125 us
  blocking collectives: 140 us -> 40.5 us
  local copies, waits for them, and re-layouts: 77.4 us -> 36.3 us
  other arithmetic: 49 us -> 15.4 us
  matrix products: 60.8 us -> 70.2 us
    all_gather x1 -> x2, waiting for transfers between devices: 241 us -> 58.5 us  [the longest x1 33.5 us: per_device(): parts = lax.all_gather(projected, 'req').astype(jnp.float32)]
    all_to_all x1 -> x0, blocking collectives: 86.1 us -> none  [per_device(): lax.all_to_all(outgoing, 'ep', split_axis=0, concat_axis=0, tiled=True)]
    all_to_all x1 -> x0, waiting for transfers between devices: 57.5 us -> none  [per_device(): lax.all_to_all(result.astype(jnp.bfloat16), 'ep', split_axis=0, concat_ax...]
    reduce_scatter x1 -> x2, waiting for transfers between devices: 16 us -> 66.3 us  [the longest x1 45.8 us: per_device(): lax.psum_scatter(term.astype(jnp.bfloat16), 'ep', scatter_dimension=0, ti...]
    gather x7 -> x0, local copies, waits for them, and re-layouts: 24.4 us -> none  [the longest x1 11.8 us: per_device(): returned.reshape(expert_total * capacity, -1)[placement]]
    add x6 -> x0, other arithmetic: 15.5 us -> none  [the longest x3 15.4 us: combine_states(): left_state[2] * left_factor[..., None]]
    all_gather x2, blocking collectives: 37.3 us -> 24.7 us  [the longest x1 15.4 us: per_device(): stats = lax.all_gather(jnp.stack([highest_score, totals]), 'req')]
    dot_general x4 -> x5, matrix products: 24.9 us -> 35.6 us  [the longest x2 20.8 us: per_device(): jnp.dot(hidden_rows, expert_down[e], preferred_element_type=jnp.float32)]
  transfers between devices with their start and end apart: 3 -> 4, of which waited for: 3 -> 4; matrix products, arithmetic and copies ran while one was open for 4% -> 3% of each run, Pallas kernels for 0% -> 0%
where the time goes in v1:
time: 302 us
  waiting for transfers between devices  125 us (41%)
  matrix products  70.2 us (23%)
  blocking collectives  40.5 us (13%)
  local copies, waits for them, and re-layouts  36.3 us (12%)
  other arithmetic  15.4 us (5%)
  between operations  14.2 us (5%)
    reduce_scatter x1, waiting for transfers between devices, per_device(): lax.psum_scatter(term.astype(jnp.bfloat16), 'ep', scatter_dimension=0, ti...  45.8 us
    all_gather x1, waiting for transfers between devices, per_device(): parts = lax.all_gather(projected, 'req').astype(jnp.float32)  33.5 us
    all_gather x1, waiting for transfers between devices, per_device(): everyone = lax.all_gather(normed, 'ep', axis=0, tiled=True)  25 us
    dot_general x2, matrix products, per_device(): jnp.dot(hidden_rows, expert_down[e], preferred_element_type=jnp.float32)  20.8 us
    reduce_scatter x1, waiting for transfers between devices, per_device(): lax.psum_scatter((shared_part + routed).astype(jnp.bfloat16), 'req', scat...  20.5 us
    all_gather x1, blocking collectives, per_device(): resid = lax.all_gather(resid_cols, 'req', axis=1, tiled=True)  15.8 us
    all_gather x1, blocking collectives, per_device(): stats = lax.all_gather(jnp.stack([highest_score, totals]), 'req')  15.4 us
    dot_general x2, matrix products, per_device(): jnp.dot(everyone, expert_gate_up[e, 0], preferred_element_type=jnp.float32)  9.82 us
  transfers between devices with their start and end apart: 4, of which 4 were waited for; matrix products, arithmetic and copies ran while one was open for 3% of the time, Pallas kernels for 0%

profile of v1, /device:TPU:0, one launch (start us, length us, event | category | flops | bytes accessed | tf_op | source)
XLA Modules:
  0.0 301.6 jit_solution(17149735106000106819)
XLA Ops:
  7.3 1.2 copy.169
  8.7 2.5 convert_bitcast_fusion
  11.2 1.6 pad_maximum_fusion
  12.9 4.9 %copy.160 = bf16[128,16,576]{2,1,0:T(8,128)(2,1)} copy(bf16[128,16,576]{0,2,1:T(8,128)(2,1)} %pad_maximum_fusion) | data formatting | bytes 4718592 | tf_op jit(solution)/shard_map/concatenate | solution.py:73
  18.5 5.6 %fusion.89 = f32[2,64,16,16]{2,3,1,0:T(8,128)S(1)} fusion(bf16[2,64,16,576]{3,2,1,0:T(8,128)(2,1)} %bitcast.150, bf16[16,2,576]{2,1,0:T(2,128)(2,1)S(1)} %gather_fusion.3, pred[16]{0:T(512)(128)(4,1)S(1)} %compare_and_fusion.1), kind=kOutput, calls=%fused_computation.109 | convolution fusion | flops 37767168 | bytes 2527248 | tf_op jit(solution)/shard_map/rthk,rsk->rths/dot_general | solution.py:81
  24.1 1.2 copy.172
  29.4 2.3 gather_fusion.1
  31.7 4.6 %copy.163 = bf16[16,128,576]{1,0,2:T(8,128)(2,1)} copy(bf16[16,128,576]{1,2,0:T(8,128)(2,1)} %gather_fusion.1) | data formatting | bytes 4718592 | tf_op jit(solution)/shard_map/gather | solution.py:60
  36.3 5.7 %reshape.287 = bf16[2,1024,576]{1,0,2:T(2,128)(2,1)} reshape(bf16[16,128,576]{1,0,2:T(8,128)(2,1)} %copy.163) | data formatting | bytes 4718592 | tf_op jit(solution)/shard_map/reshape | solution.py:60
  42.1 4.5 %slice.79 = bf16[2,1024,512]{1,0,2:T(2,128)(2,1)} slice(bf16[2,1024,576]{1,0,2:T(2,128)(2,1)} %reshape.287), slice={[0:2], [0:1024], [0:512]} | slice | bytes 4194304 | tf_op jit(solution)/shard_map/slice | solution.py:96
  46.7 8.0 %fusion = (f32[2,64,16]{2,1,0:T(8,128)S(1)}, f32[2,64,16,1024]{3,2,1,0:T(8,128)}) fusion(pred[2,1024]{1,0:T(4,128)(4,1)S(1)} %broadcast_compare_fusion, bf16[2,64,16,576]{3,2,1,0:T(8,128)(2,1)S(1)} %bitcast.151, bf16[2,1024,576,1]{1,0,2,3:T(2,128)(2,1)} %bitcast.152), kind=kOutput, calls=%fused_computation.10 | convolution fusion | flops 2422208512 | bytes 13117440 | tf_op jit(solution)/shard_map/rthk,rsk->rths/dot_general | solution.py:76
  55.0 5.9 %fusion.1 = (f32[2,64,16]{2,1,0:T(8,128)S(1)}, bf16[2,64,16,1024]{3,2,1,0:T(8,128)(2,1)}) fusion(f32[2,64,16,1024]{3,2,1,0:T(8,128)} %get-tuple-element.27, f32[2,64,16]{2,1,0:T(8,128)S(1)} %max.17, pred[2,1024]{1,0:T(4,128)(4,1)S(1)} %broadcast_compare_fusion), kind=kLoop, calls=%fused_computation.11 | loop fusion | flops 12580864 | bytes 12601344 | tf_op jit(solution)/shard_map/reduce_sum | solution.py:92
  60.9 6.1 %copy.198 = bf16[2,1024,512]{2,1,0:T(8,128)(2,1)} copy(bf16[2,1024,512]{1,0,2:T(2,128)(2,1)} %slice.79) | data formatting | bytes 4194304
  67.0 7.5 %fusion.4 = f32[2,64,16,512]{3,1,0,2:T(8,128)} fusion(bf16[2,64,16,1024]{3,2,1,0:T(8,128)(2,1)} %get-tuple-element.19, bf16[2,1024,512]{2,1,0:T(8,128)(2,1)} %copy.198), kind=kOutput, calls=%fused_computation.15 | convolution fusion | flops 2147483648 | bytes 10485760 | tf_op jit(solution)/shard_map/rths,rsl->rthl/dot_general | solution.py:93
  74.5 5.0 %fusion.44 = bf16[2,64,16,128]{3,1,0,2:T(8,128)(2,1)} fusion(bf16[16,512,128]{2,1,0:T(8,128)(2,1)} %param.27, f32[2,64,16,512]{3,1,0,2:T(8,128)} %fusion.4, bf16[2,64,16,16]{1,3,2,0:T(8,128)(2,1)S(1)} %get-tuple-element.21, bf16[2,16,576]{2,1,0:T(8,128)(2,1)S(1)} %fusion.98), kind=kOutput, calls=%fused_computation.56 | convolution fusion | flops 304349184 | bytes 6979584 | tf_op jit(solution)/shard_map/rthl,hlv->rthv/dot_general | solution.py:105
  79.8 15.4 %all-gather.1 = f32[8,2,64,16]{2,3,1,0:T(8,128)S(1)} all-gather(f32[2,2,64,16]{2,3,1,0:T(8,128)S(1)} %pad_maximum_fusion.1), channel_id=3, replica_groups=mesh['req'=4,'ep'=8] {'req'}, dimensions={0}, use_global_device_ids=true | all-gather | bytes 81920 | tf_op jit(solution)/shard_map/all_gather | solution.py:111
  95.4 33.5 %all-gather.7.cloned.1.call-done = bf16[8,64,16,128]{3,1,0,2:T(8,128)(2,1)} async-done(((bf16[2,64,16,128]{3,1,0,2:T(8,128)(2,1)}), bf16[8,64,16,128]{3,1,0,2:T(8,128)(2,1)}) %all-gather.7.cloned.1.call-update) | async-done | bytes 2097168 | tf_op jit(solution)/shard_map/all_gather | solution.py:112
  128.9 2.7 fusion.3
  132.5 15.8 %all_gather.25 = bf16[128,2048]{1,0:T(8,128)(2,1)S(1)} all-gather(bf16[128,512]{1,0:T(8,128)(2,1)S(1)} %fusion.49), channel_id=1, replica_groups=mesh['req'=4,'ep'=8] {'req'}, dimensions={1}, use_global_device_ids=true | all-gather | bytes 655360 | tf_op jit(solution)/shard_map/all_gather | solution.py:119
  149.6 1.3 fusion.112
  151.0 9.3 %all_gather.26 = f32[1024,16]{0,1:T(8,128)S(1)} all-gather(f32[128,16]{0,1:T(8,128)S(1)} %broadcast_divide_fusion), channel_id=1, replica_groups=mesh['req'=4,'ep'=8] {'ep'}, dimensions={0}, use_global_device_ids=true | all-gather | bytes 73728 | tf_op jit(solution)/shard_map/all_gather | solution.py:134
  160.2 25.0 %all-gather.5.cloned.1.call-done = bf16[1024,2048]{1,0:T(8,128)(2,1)} async-done(((bf16[128,2048]{1,0:T(8,128)(2,1)}), bf16[1024,2048]{1,0:T(8,128)(2,1)}) %all-gather.5.cloned.1.call-update) | async-done | bytes 4194320 | tf_op jit(solution)/shard_map/all_gather | solution.py:125
  185.3 5.6 %fusion.19 = f32[1024,352]{0,1:T(8,128)} fusion(bf16[1024,2048]{1,0:T(8,128)(2,1)} %all-gather.5.cloned.1.call-done, bf16[2,2,2048,352]{2,3,1,0:T(8,128)(2,1)} %param.32), kind=kOutput, calls=%fused_computation.36 | convolution fusion | flops 1476395008 | bytes 7077888 | tf_op jit(solution)/shard_map/dot_general | solution.py:144
  190.9 4.2 %fusion.14 = f32[1024,352]{0,1:T(8,128)} fusion(bf16[1024,2048]{1,0:T(8,128)(2,1)S(1)} %copy-done.15, bf16[2,2,2048,352]{2,3,1,0:T(8,128)(2,1)} %param.32), kind=kOutput, calls=%fused_computation.31 | convolution fusion | flops 1476395008 | bytes 7077888 | tf_op jit(solution)/shard_map/dot_general | solution.py:144
  195.1 10.7 %fusion.16 = f32[1024,2048]{1,0:T(8,128)} fusion(bf16[2,352,2048]{2,1,0:T(8,128)(2,1)} %param.33, bf16[1024,2048]{1,0:T(8,128)(2,1)} %all-gather.5.cloned.1.call-done, bf16[2,2,2048,352]{2,3,1,0:T(8,128)(2,1)} %param.32, f32[1024,352]{0,1:T(8,128)} %fusion.19), kind=kOutput, calls=%fused_computation.33 | convolution fusion | flops 2954952704 | bytes 16908288 | tf_op jit(solution)/shard_map/dot_general | solution.py:151
  205.7 10.1 %add_convert_fusion = bf16[1024,2048]{1,0:T(8,128)(2,1)} fusion(f32[1024,2048]{1,0:T(8,128)} %fusion.16, f32[1024]{0:T(1024)S(1)} %bitcast.165, f32[1024]{0:T(1024)S(1)} %bitcast.164, bf16[2,352,2048]{2,1,0:T(8,128)(2,1)} %param.33, bf16[1024,2048]{1,0:T(8,128)(2,1)} %all-gather.5.cloned.1.call-done, bf16[2,2,2048,352]{2,3,1,0:T(8,128)(2,1)} %param.32, ...), kind=kOutput, calls=%fused_computation.7 | convolution fusion | flops 2963341312 | bytes 21110784 | tf_op jit(solution)/shard_map/dot_general | solution.py:151
  219.0 2.6 fusion.23
  221.6 45.8 %reduce-scatter.3.cloned.1.call-done = bf16[128,2048]{1,0:T(8,128)(2,1)} async-done(((bf16[1024,2048]{1,0:T(8,128)(2,1)}), bf16[128,2048]{1,0:T(8,128)(2,1)}) %reduce-scatter.3.cloned.1.call-update) | async-done | bytes 524304 | tf_op jit(solution)/shard_map/reduce_scatter | solution.py:153
  267.4 4.3 %fusion.6 = bf16[128,2048]{1,0:T(8,128)(2,1)} fusion(bf16[352,2048]{1,0:T(8,128)(2,1)} %param.35, bf16[128,2048]{1,0:T(8,128)(2,1)S(1)} %copy-done.3, bf16[2,2048,352]{1,2,0:T(8,128)(2,1)} %param.34, bf16[128,2048]{1,0:T(8,128)(2,1)} %reduce-scatter.3.cloned.1.call-done, f32[128,352]{0,1:T(8,128)} %fusion.23), kind=kOutput, calls=%fused_computation.19 | convolution fusion | flops 370155520 | bytes 4636672 | tf_op jit(solution)/shard_map/dot_general | solution.py:141
  271.9 1.1 fusion.48
  273.0 20.5 %reduce-scatter.5.cloned.1.call-done = bf16[128,512]{1,0:T(8,128)(2,1)} async-done(((bf16[128,2048]{1,0:T(8,128)(2,1)}), bf16[128,512]{1,0:T(8,128)(2,1)}) %reduce-scatter.5.cloned.1.call-update) | async-done | bytes 131088 | tf_op jit(solution)/shard_map/reduce_scatter | solution.py:156
  293.5 1.6 add_convert_fusion.2
  (112 shorter events, 11.2 us)
Async XLA Ops:
  7.2 22.2 %copy-start = (bf16[16,128,576]{1,2,0:T(8,128)(2,1)S(1)}, bf16[16,128,576]{1,2,0:T(8,128)(2,1)}, u32[]{:S(2)}) copy-start(bf16[16,128,576]{1,2,0:T(8,128)(2,1)} %param.21) | copy-start | bytes 7077892
  7.2 121.7 %all-gather.7.cloned.1.call-start = ((), (), s32[]{:S(2)}) async-start(), calls=%async_computation.5 | async-start | bytes 2621440 | tf_op jit(solution)/shard_map/all_gather | solution.py:112
  8.5 2.7 copy-start.6
  8.7 2.5 slice-start
  17.8 7.5 %copy-start.13 = (s32[2,64]{1,0:T(2,128)S(1)}, s32[2,64]{1,0:T(2,128)}, u32[]{:S(2)}) copy-start(s32[2,64]{1,0:T(2,128)} %param.24) | copy-start | bytes 1540
  18.5 10.1 %copy-start.1 = (s32[2,32]{1,0:T(2,128)S(1)}, s32[2,32]{1,0:T(2,128)}, u32[]{:S(2)}) copy-start(s32[2,32]{1,0:T(2,128)} %param.22) | copy-start | bytes 772
  42.0 4.6 %copy-start.11 = (s32[2]{0:T(128)S(1)}, s32[2]{0:T(128)}, u32[]{:S(2)}) copy-start(s32[2]{0:T(128)} %param.23) | copy-start | bytes 28
  42.0 4.7 %copy-start.2 = (bf16[128,16,576]{2,1,0:T(8,128)(2,1)S(1)}, bf16[128,16,576]{2,1,0:T(8,128)(2,1)}, u32[]{:S(2)}) copy-start(bf16[128,16,576]{2,1,0:T(8,128)(2,1)} %copy.160) | copy-start | bytes 7077892
  46.7 8.1 %copy-start.4 = (f32[2,64,16,16]{1,3,2,0:T(8,128)S(1)}, f32[2,64,16,16]{1,3,2,0:T(8,128)}, u32[]{:S(2)}) copy-start(f32[2,64,16,16]{1,3,2,0:T(8,128)} %copy.172) | copy-start | bytes 393220
  79.5 52.5 %copy-start.8 = (bf16[128,512]{1,0:T(8,128)(2,1)S(1)}, bf16[128,512]{1,0:T(8,128)(2,1)}, u32[]{:S(2)}) copy-start(bf16[128,512]{1,0:T(8,128)(2,1)} %param.20) | copy-start | bytes 393220
  79.5 105.7 %all-gather.5.cloned.1.call-start = ((), (), s32[]{:S(2)}) async-start(), calls=%async_computation.2 | async-start | bytes 4718592 | tf_op jit(solution)/shard_map/all_gather | solution.py:125
  128.9 3.1 %copy-start.5 = (bf16[2048,512]{1,0:T(8,128)(2,1)S(1)}, bf16[2048,512]{1,0:T(8,128)(2,1)}, u32[]{:S(2)}) copy-start(bf16[2048,512]{1,0:T(8,128)(2,1)} %param.28) | copy-start | bytes 6291460
  131.6 16.9 %copy-start.10 = (f32[2048]{0:T(1024)S(1)}, f32[2048]{0:T(1024)}, u32[]{:S(2)}) copy-start(f32[2048]{0:T(1024)} %param.29) | copy-start | bytes 24580
  132.0 17.6 %copy-start.12 = (s32[128,6]{0,1:T(8,128)S(1)}, s32[128,6]{0,1:T(8,128)}, u32[]{:S(2)}) copy-start(s32[128,6]{0,1:T(8,128)} %param.31) | copy-start | bytes 9220
  132.0 17.6 %copy-start.9 = (bf16[2048,16]{0,1:T(8,128)(2,1)S(1)}, bf16[2048,16]{0,1:T(8,128)(2,1)}, u32[]{:S(2)}) copy-start(bf16[2048,16]{0,1:T(8,128)(2,1)} %param.30) | copy-start | bytes 196612
  149.5 117.9 %reduce-scatter.3.cloned.1.call-start = ((), (), s32[]{:S(2)}) async-start(), calls=%async_computation.3 | async-start | bytes 4718592 | tf_op jit(solution)/shard_map/reduce_scatter | solution.py:153
  185.3 5.6 %copy-start.15 = (bf16[1024,2048]{1,0:T(8,128)(2,1)S(1)}, bf16[1024,2048]{1,0:T(8,128)(2,1)}, u32[]{:S(2)}) copy-start(bf16[1024,2048]{1,0:T(8,128)(2,1)} %all-gather.5.cloned.1.call-done) | copy-start | bytes 12582916
  215.9 0.7 copy-start.14
  215.9 3.2 %copy-start.3 = (bf16[128,2048]{1,0:T(8,128)(2,1)S(1)}, bf16[128,2048]{1,0:T(8,128)(2,1)}, u32[]{:S(2)}) copy-start(bf16[128,2048]{1,0:T(8,128)(2,1)} %fusion.64) | copy-start | bytes 1572868
  215.9 77.6 %reduce-scatter.5.cloned.1.call-start = ((), (), s32[]{:S(2)}) async-start(), calls=%async_computation.4 | async-start | bytes 655360 | tf_op jit(solution)/shard_map/reduce_scatter | solution.py:156
  221.6 50.3 %copy-start.7 = (bf16[128,576]{1,0:T(8,128)(2,1)S(1)}, bf16[128,576]{1,0:T(8,128)(2,1)}, u32[]{:S(2)}) copy-start(bf16[128,576]{1,0:T(8,128)(2,1)} %copy-done.6) | copy-start | bytes 442372
Sparse Core Ops, SparseCore 0:
  79.7 49.1 all-gather.6
  149.7 35.5 all-gather.4
  216.0 51.3 reduce-scatter.2
  271.8 21.6 reduce-scatter.4

commit v2 on v1

v2 whole, which is shorter than its diff:
```python
import functools
import math

import jax
import jax.numpy as jnp
from jax import lax
from jax.experimental import pallas as pl
from jax.experimental.pallas import tpu as pltpu
from jax.sharding import PartitionSpec as P

NEGATIVE = -1e30
FLOOR = -1e29
MESH = pl.DeviceIdType.MESH


DRAFT_PAD = 128


def attend_kernel(scale, page_count, slots, absorbed, rotary, *rest):
    pages = rest[:page_count]
    drafts, cache_bias, tree_bias, value, projected, peaks, sums, keys, bias = rest[page_count:]
    page_size = pages[0].shape[1]
    cached = page_count * page_size
    draft_count = drafts.shape[1]
    latent_width = absorbed.shape[2]
    head_count = absorbed.shape[0]
    group = head_count // projected.shape[0]
    value_width = value.shape[2]
    for p in range(page_count):
        keys[p * page_size : (p + 1) * page_size, :] = pages[p][0]
    keys[cached : cached + draft_count, :] = drafts[0]
    keys[cached + draft_count :, :] = jnp.zeros(
        (DRAFT_PAD - draft_count, keys.shape[1]), keys.dtype
    )
    bias[:, :cached] = jnp.broadcast_to(cache_bias[0], (draft_count, cached))
    bias[:, cached:] = tree_bias[0]
    contract_last = (((1,), (1,)), ((), ()))
    peaks[...] = jnp.zeros_like(peaks)
    sums[...] = jnp.ones_like(sums)

    for chunk in range(head_count // group):
        rows = slice(chunk * group, (chunk + 1) * group)
        nope = absorbed[rows].reshape(group * draft_count, latent_width)
        rope = rotary[rows].reshape(group * draft_count, rotary.shape[2])
        scores = lax.dot_general(
            nope, keys[:, :latent_width], contract_last, preferred_element_type=jnp.float32
        ) + lax.dot_general(
            rope, keys[:, latent_width:], contract_last, preferred_element_type=jnp.float32
        )
        scores = scores.reshape(group, draft_count, -1) * scale + bias[...][None]
        scores = scores.reshape(group * draft_count, -1)
        peak = jnp.maximum(jnp.max(scores, axis=1, keepdims=True), FLOOR)
        weights = jnp.exp(scores - peak)
        total = jnp.sum(weights, axis=1, keepdims=True)
        mixed = jnp.dot(
            weights.astype(jnp.bfloat16), keys[:, :latent_width],
            preferred_element_type=jnp.float32,
        ).astype(jnp.bfloat16)
        for j in range(group):
            h = chunk * group + j
            own = slice(j * draft_count, (j + 1) * draft_count)
            projected[chunk, :, j * value_width : (j + 1) * value_width] = jnp.dot(
                mixed[own], value[h], preferred_element_type=jnp.float32
            ).astype(jnp.bfloat16)
            peaks[:, h : h + 1] = peak[own]
            sums[:, h : h + 1] = total[own]


def attend(slots, absorbed, rotary, pool, drafts, cache_bias, tree_bias, value, scale, chunks):
    requests, page_count = slots.shape
    heads, tokens, latent_width = absorbed.shape
    page_size, key_width = pool.shape[1:]
    draft_count = drafts.shape[1]
    width = heads // chunks * value.shape[2]
    cached = page_count * page_size

    def page_spec(p):
        return pl.BlockSpec((1, page_size, key_width), lambda r, table: (table[r, p], 0, 0))

    def by_request(shape):
        return pl.BlockSpec((1,) + shape, lambda r, table: (r, 0, 0))

    return pl.pallas_call(
        functools.partial(attend_kernel, scale, page_count),
        grid_spec=pltpu.PrefetchScalarGridSpec(
            num_scalar_prefetch=1,
            grid=(requests,),
            in_specs=[
                pl.BlockSpec((heads, draft_count, latent_width), lambda r, table: (0, r, 0)),
                pl.BlockSpec((heads, draft_count, rotary.shape[2]), lambda r, table: (0, r, 0)),
                *[page_spec(p) for p in range(page_count)],
                by_request((draft_count, key_width)),
                by_request((1, cached)),
                by_request((draft_count, DRAFT_PAD)),
                pl.BlockSpec(value.shape, lambda r, table: (0, 0, 0)),
            ],
            out_specs=[
                pl.BlockSpec((chunks, draft_count, width), lambda r, table: (0, r, 0)),
                pl.BlockSpec((draft_count, 128), lambda r, table: (r, 0)),
                pl.BlockSpec((draft_count, 128), lambda r, table: (r, 0)),
            ],
            scratch_shapes=[
                pltpu.VMEM((cached + DRAFT_PAD, key_width), jnp.bfloat16),
                pltpu.VMEM((draft_count, cached + DRAFT_PAD), jnp.float32),
            ],
        ),
        out_shape=[
            jax.ShapeDtypeStruct((chunks, tokens, width), jnp.bfloat16),
            jax.ShapeDtypeStruct((tokens, 128), jnp.float32),
            jax.ShapeDtypeStruct((tokens, 128), jnp.float32),
        ],
        compiler_params=pltpu.CompilerParams(vmem_limit_bytes=40 * 1024 * 1024),
    )(slots, absorbed, rotary, *[pool] * page_count, drafts, cache_bias, tree_bias, value)


def exchange_kernel(
    n_req, n_ep, parts, stats, hidden, out_proj_hbm, gain, router, named, gate_up_hbm, down_hbm,
    shared_up_hbm, shared_down_hbm, out,
    out_proj, gate_up, down, shared_up, shared_down, weight_sem,
    part_in, stat_in, head_in, resid_in, final_out, final_in, z_send, z_recv,
    rows, gates, mate_out, mate_in, back_out, back_in, total,
    row_send, row_recv, fwd_send, fwd_recv, mate_send, mate_recv, back_send, back_recv,
):
    f32, bf16 = jnp.float32, jnp.bfloat16
    req = lax.axis_index("req")
    ep = lax.axis_index("ep")
    chips = n_ep // 2
    core = ep % 2
    chip = ep // 2
    mate = chip * 2 + 1 - core
    tokens, width = hidden.shape
    group = stats.shape[1] // 2
    value_width = width // group
    expert_total = named.shape[1]
    local_experts = gate_up.shape[0]

    def partner(s):
        there, bit = 0, 1
        while bit < chips:
            there = there + bit * (((chip // bit) % 2 + (s // bit) % 2) % 2)
            bit *= 2
        return there * 2 + core

    loads = [
        pltpu.make_async_copy(src, dst, weight_sem.at[i])
        for i, (src, dst) in enumerate(
            [
                (out_proj_hbm, out_proj),
                (shared_up_hbm, shared_up),
                (shared_down_hbm, shared_down),
                (gate_up_hbm, gate_up),
                (down_hbm, down),
            ]
        )
    ]
    for load in loads:
        load.start()

    barrier = pltpu.get_barrier_semaphore()
    for delta in range(1, n_req):
        pl.semaphore_signal(
            barrier, inc=1, device_id=((req + delta) % n_req, ep), device_id_type=MESH
        )
    for s in range(1, chips):
        pl.semaphore_signal(barrier, inc=1, device_id=(req, partner(s)), device_id_type=MESH)
    pl.semaphore_signal(barrier, inc=1, device_id=(req, mate), device_id_type=MESH)
    pl.semaphore_wait(barrier, n_req - 1 + chips)

    def along_z(stage, delta, src, dst):
        return pltpu.make_async_remote_copy(
            src_ref=src, dst_ref=dst,
            send_sem=z_send.at[stage, delta], recv_sem=z_recv.at[stage, delta],
            device_id=((req + delta) % n_req, ep), device_id_type=MESH,
        )

    sent = []
    for delta in range(1, n_req):
        to = (req + delta) % n_req
        sent.append(along_z(0, delta, parts.at[to], part_in.at[delta]))
        sent.append(along_z(1, delta, stats.at[to], stat_in.at[delta]))
    for copy in sent:
        copy.start()
    part_in[0] = parts[req]
    stat_in[0] = stats[req]
    for copy in sent:
        copy.wait()

    flat = stat_in[...].reshape(n_req * 2 * group, tokens)
    flat = jnp.concatenate([flat, jnp.zeros((128 - flat.shape[0], tokens), f32)], axis=0)
    columns = flat.T
    for j in range(group):
        at = [d * 2 * group + j for d in range(n_req)]
        peak = [columns[:, i : i + 1] for i in at]
        total_at = [columns[:, i + group : i + group + 1] for i in at]
        top = functools.reduce(jnp.maximum, peak)
        factor = [jnp.exp(p - top) for p in peak]
        inverse = 1.0 / sum(f * t for f, t in zip(factor, total_at))
        lanes = slice(j * value_width, (j + 1) * value_width)
        head = sum(
            part_in[d, :, lanes].astype(f32) * (factor[d] * inverse) for d in range(n_req)
        )
        head_in[0, :, lanes] = head.astype(bf16)

    sent = [along_z(2, d, head_in.at[0], head_in.at[d]) for d in range(1, n_req)]
    for copy in sent:
        copy.start()
    loads[0].wait()

    def project(delta):
        src = (req + n_req - delta) % n_req
        return jnp.dot(
            head_in[delta], out_proj[pl.ds(pl.multiple_of(src * width, width), width), :],
            preferred_element_type=f32,
        )

    attention = project(0)
    for d in range(1, n_req):
        sent[d - 1].wait()
        attention = attention + project(d)
    own_resid = (hidden[...].astype(f32) + attention).astype(bf16)
    resid_in[req] = own_resid
    sent = [along_z(3, d, resid_in.at[req], resid_in.at[req]) for d in range(1, n_req)]
    for copy in sent:
        copy.start()
    for copy in sent:
        copy.wait()

    square = 0.0
    for d in range(n_req):
        wide = resid_in[d].astype(f32)
        square = square + jnp.sum(wide * wide, axis=1, keepdims=True)
    inverse = lax.rsqrt(square / (n_req * width) + 1e-06)
    for d in range(n_req):
        lanes = slice(d * width, (d + 1) * width)
        rows[0, 0, :, lanes] = (
            resid_in[d].astype(f32) * inverse * gain[:, lanes]
        ).astype(bf16)
    logits = jnp.dot(rows[0, 0], router[...], preferred_element_type=f32)
    lifted = named[...] / (1.0 + jnp.exp(-logits))
    gate = lifted / jnp.sum(lifted, axis=1, keepdims=True)
    gate = jnp.concatenate([gate, jnp.zeros((tokens, 128 - expert_total), f32)], axis=1)
    gates[0, 0] = gate.T[:expert_total]

    def spread(s):
        to = (req, partner(s))
        return [
            pltpu.make_async_remote_copy(
                src_ref=buf.at[0, 0], dst_ref=buf.at[s, 0],
                send_sem=row_send.at[s, i], recv_sem=row_recv.at[s, i],
                device_id=to, device_id_type=MESH,
            )
            for i, buf in enumerate((rows, gates))
        ]

    def forward(s):
        return [
            pltpu.make_async_remote_copy(
                src_ref=buf.at[s, 0], dst_ref=buf.at[s, 1],
                send_sem=fwd_send.at[s, i], recv_sem=fwd_recv.at[s, i],
                device_id=(req, mate), device_id_type=MESH,
            )
            for i, buf in enumerate((rows, gates))
        ]

    def to_mate(s):
        return pltpu.make_async_remote_copy(
            src_ref=mate_out.at[s], dst_ref=mate_in.at[s],
            send_sem=mate_send.at[s], recv_sem=mate_recv.at[s],
            device_id=(req, mate), device_id_type=MESH,
        )

    def send_back(s):
        return pltpu.make_async_remote_copy(
            src_ref=back_out.at[s], dst_ref=back_in.at[s],
            send_sem=back_send.at[s], recv_sem=back_recv.at[s],
            device_id=(req, partner(s)), device_id_type=MESH,
        )

    for s in range(1, chips):
        for copy in spread(s):
            copy.start()
    for copy in forward(0):
        copy.start()

    def silu_times(value, lift):
        return value / (1.0 + jnp.exp(-value)) * lift

    loads[1].wait()
    loads[2].wait()
    shared_hidden = silu_times(
        jnp.dot(rows[0, 0], shared_up[0], preferred_element_type=f32),
        jnp.dot(rows[0, 0], shared_up[1], preferred_element_type=f32),
    ).astype(bf16)
    total[...] = jnp.dot(shared_hidden, shared_down[...], preferred_element_type=f32)
    loads[3].wait()
    loads[4].wait()

    def step(s, carry):
        @pl.when(s > 0)
        def _():
            for copy in spread(s):
                copy.wait_recv()
            for copy in forward(s):
                copy.start()

        for copy in forward(s):
            copy.wait_recv()
        both = rows[s].reshape(2 * tokens, n_req * width)
        own_gate = []
        for k in range(2):
            flat = gates[s, k]
            flat = jnp.concatenate([flat, jnp.zeros((128 - expert_total, tokens), f32)], axis=0)
            own_gate.append(flat.T)
        own_gate = jnp.concatenate(own_gate, axis=0)
        lane = lax.broadcasted_iota(jnp.int32, own_gate.shape, 1)
        weighted = []
        for e in range(local_experts):
            column = jnp.sum(
                jnp.where(lane == ep * local_experts + e, own_gate, 0.0), axis=1, keepdims=True
            )
            hidden_rows = silu_times(
                jnp.dot(both, gate_up[e, 0], preferred_element_type=f32),
                jnp.dot(both, gate_up[e, 1], preferred_element_type=f32),
            )
            weighted.append((hidden_rows * column).astype(bf16))

        def result(k):
            return sum(
                jnp.dot(
                    weighted[e][k * tokens : (k + 1) * tokens], down[e],
                    preferred_element_type=f32,
                )
                for e in range(local_experts)
            )

        mate_out[s] = result(1).astype(bf16)
        to_mate(s).start()
        own = result(0)
        to_mate(s).wait_recv()
        own = own + mate_in[s].astype(f32)

        @pl.when(s == 0)
        def _():
            total[...] += own

        @pl.when(s > 0)
        def _():
            back_out[s] = own.astype(bf16)
            send_back(s).start()

        return carry

    lax.fori_loop(0, chips, step, 0)
    summed = total[...]
    for s in range(1, chips):
        send_back(s).wait_recv()
        summed = summed + back_in[s].astype(f32)
    total[...] = summed
    for d in range(n_req):
        final_out[d] = summed[:, d * width : (d + 1) * width].astype(bf16)
    sent = []
    for delta in range(1, n_req):
        to = (req + delta) % n_req
        sent.append(along_z(4, delta, final_out.at[to], final_in.at[delta]))
    for copy in sent:
        copy.start()
    for s in range(chips):
        for copy in forward(s):
            copy.wait_send()
        to_mate(s).wait_send()
        if s:
            for copy in spread(s):
                copy.wait_send()
            send_back(s).wait_send()
    answer = resid_in[req].astype(f32) + final_out[req].astype(f32)
    for d in range(1, n_req):
        sent[d - 1].wait()
        answer = answer + final_in[d].astype(f32)
    out[...] = answer.astype(bf16)


def exchange(
    parts, stats, hidden, out_proj, gain, router, named, gate_up, down, shared_up, shared_down,
    n_req, n_ep,
):
    tokens, width = hidden.shape
    model = n_req * width
    chips = n_ep // 2
    bf16, f32 = jnp.bfloat16, jnp.float32
    in_vmem = pl.BlockSpec(memory_space=pltpu.VMEM)
    in_any = pl.BlockSpec(memory_space=pl.ANY)
    dma = pltpu.SemaphoreType.DMA
    weights = [out_proj, gate_up, down, shared_up, shared_down]
    return pl.pallas_call(
        functools.partial(exchange_kernel, n_req, n_ep),
        out_shape=jax.ShapeDtypeStruct((tokens, width), bf16),
        in_specs=[in_vmem] * 3 + [in_any] + [in_vmem] * 3 + [in_any] * 4,
        out_specs=in_vmem,
        scratch_shapes=[
            *[pltpu.VMEM(w.shape, w.dtype) for w in weights],
            dma((5,)),
            pltpu.VMEM(parts.shape, bf16),
            pltpu.VMEM(stats.shape, f32),
            pltpu.VMEM((n_req, tokens, width), bf16),
            pltpu.VMEM((n_req, tokens, width), bf16),
            pltpu.VMEM((n_req, tokens, width), bf16),
            pltpu.VMEM((n_req, tokens, width), bf16),
            dma((5, n_req)),
            dma((5, n_req)),
            pltpu.VMEM((chips, 2, tokens, model), bf16),
            pltpu.VMEM((chips, 2, named.shape[1], tokens), f32),
            pltpu.VMEM((chips, tokens, model), bf16),
            pltpu.VMEM((chips, tokens, model), bf16),
            pltpu.VMEM((chips, tokens, model), bf16),
            pltpu.VMEM((chips, tokens, model), bf16),
            pltpu.VMEM((tokens, model), f32),
            dma((chips, 2)),
            dma((chips, 2)),
            dma((chips, 2)),
            dma((chips, 2)),
            dma((chips,)),
            dma((chips,)),
            dma((chips,)),
            dma((chips,)),
        ],
        compiler_params=pltpu.CompilerParams(
            collective_id=0, has_side_effects=True, vmem_limit_bytes=56 * 1024 * 1024
        ),
    )(parts, stats, hidden, out_proj, gain, router, named, gate_up, down, shared_up, shared_down)


def ancestors(parents):
    draft_count = parents.shape[-1]
    draft_index = jnp.arange(draft_count, dtype=jnp.int32)
    ancestry = (parents[:, :, None] == draft_index[None, None, :]).astype(jnp.float32)
    ancestry = ancestry + jnp.eye(draft_count, dtype=jnp.float32)[None]
    for doubling in range(max(1, (draft_count - 1).bit_length())):
        ancestry = jnp.minimum(
            jnp.einsum("rij,rjk->rik", ancestry, ancestry, precision=lax.Precision.HIGHEST), 1.0
        )
    return ancestry


def per_device(
    queries,
    draft_latent,
    hidden_in,
    cache_pool,
    page_table,
    cache_len,
    parents,
    accept_leaf,
    absorb_key,
    absorb_value,
    out_proj,
    norm_gain,
    router,
    expert_ids,
    expert_gate_up,
    expert_down,
    shared_gate_up,
    shared_down,
):
    req_count = lax.axis_size("req")
    req_index = lax.axis_index("req")
    ep_count = lax.axis_size("ep")
    request_count, draft_count = parents.shape
    token_count = request_count * draft_count
    head_count = queries.shape[1]
    nope_width = absorb_key.shape[1]
    latent_width = absorb_key.shape[2]
    page_size = cache_pool.shape[1]
    key_width = cache_pool.shape[2]
    page_count = page_table.shape[1]
    score_scale = 1.0 / math.sqrt(queries.shape[2])
    ancestry = ancestors(parents)
    depths = jnp.sum(ancestry, axis=2) - 1.0
    local_pages = page_count // req_count
    page_cols = req_index + req_count * jnp.arange(local_pages, dtype=jnp.int32)
    slot_rows = jnp.take(page_table, page_cols, axis=1)
    positions = (
        page_cols[:, None] * page_size + jnp.arange(page_size, dtype=jnp.int32)[None, :]
    ).reshape(-1)
    cache_bias = jnp.where(positions[None, :] < cache_len[:, None], 0.0, NEGATIVE)[:, None, :]
    draft_share = draft_count // req_count
    draft_index = jnp.arange(draft_count, dtype=jnp.int32)
    own_draft = draft_index // draft_share == req_index
    tree_bias = jnp.where((ancestry > 0.5) & own_draft[None, None, :], 0.0, NEGATIVE)
    tree_bias = jnp.pad(
        tree_bias, ((0, 0), (0, 0), (0, DRAFT_PAD - draft_count)), constant_values=NEGATIVE
    )
    own_latent = draft_latent.reshape(request_count, draft_count, key_width)
    absorbed = jnp.einsum(
        "thd,hdl->htl", queries[:, :, :nope_width], absorb_key, preferred_element_type=jnp.float32
    ).astype(jnp.bfloat16)
    rotary = jnp.transpose(queries[:, :, nope_width:], (1, 0, 2))
    projected, peaks, sums = attend(
        slot_rows, absorbed, rotary, cache_pool, own_latent, cache_bias, tree_bias, absorb_value,
        score_scale, req_count,
    )
    local_experts = expert_gate_up.shape[0]
    expert_total = local_experts * ep_count
    named = jnp.any(
        expert_ids[:, :, None] == jnp.arange(expert_total, dtype=jnp.int32)[None, None, :], axis=1
    ).astype(jnp.float32)
    if ep_count <= 8:
        group = head_count // req_count
        by_head = jnp.stack([peaks[:, :head_count].T, sums[:, :head_count].T])
        by_head = by_head.reshape(2, req_count, group, token_count)
        by_head = jnp.transpose(by_head, (1, 0, 2, 3)).reshape(req_count, 2 * group, token_count)
        layer_out = exchange(
            projected, by_head, hidden_in, out_proj, norm_gain.reshape(1, -1), router, named,
            expert_gate_up, expert_down, shared_gate_up, shared_down, req_count, ep_count,
        )
    else:
        stats = lax.all_gather(jnp.stack([peaks, sums]), "req")
        parts = lax.all_gather(projected, "req").astype(jnp.float32)
        factors = jnp.exp(stats[:, 0] - jnp.max(stats[:, 0], axis=0)[None])
        factors = factors / jnp.sum(factors * stats[:, 1], axis=0)[None]
        factors = jnp.transpose(factors[..., :head_count], (0, 2, 1))
        parts = parts.reshape(req_count, req_count, token_count, head_count // req_count, -1)
        parts = jnp.transpose(parts, (0, 1, 3, 2, 4)).reshape(req_count, head_count, token_count, -1)
        head_out = jnp.transpose(jnp.sum(parts * factors[..., None], axis=0), (1, 0, 2))
        head_rows = head_out.astype(jnp.bfloat16).reshape(token_count, -1)
        attention = jnp.dot(head_rows, out_proj, preferred_element_type=jnp.float32)
        resid_cols = (hidden_in.astype(jnp.float32) + attention).astype(jnp.bfloat16)
        resid = lax.all_gather(resid_cols, "req", axis=1, tiled=True)
        resid_wide = resid.astype(jnp.float32)
        normed = resid_wide * lax.rsqrt(
            jnp.mean(resid_wide * resid_wide, axis=1, keepdims=True) + 1e-06
        )
        normed = (normed * norm_gain[None, :]).astype(jnp.bfloat16)
        everyone = lax.all_gather(normed, "ep", axis=0, tiled=True)
        logits = jnp.dot(normed, router, preferred_element_type=jnp.float32)
        lifted = jax.nn.sigmoid(logits) * named
        gates = lifted / jnp.sum(lifted, axis=1, keepdims=True)
        gates_all = lax.all_gather(gates, "ep", axis=0, tiled=True)
        own_gates = lax.dynamic_slice_in_dim(
            gates_all, lax.axis_index("ep") * local_experts, local_experts, axis=1
        )
        shared_gate = jnp.dot(normed, shared_gate_up[0], preferred_element_type=jnp.float32)
        shared_lift = jnp.dot(normed, shared_gate_up[1], preferred_element_type=jnp.float32)
        shared_hidden = (jax.nn.silu(shared_gate) * shared_lift).astype(jnp.bfloat16)
        shared_part = jnp.dot(shared_hidden, shared_down, preferred_element_type=jnp.float32)
        term = 0.0
        for e in range(local_experts):
            gate_value = jnp.dot(
                everyone, expert_gate_up[e, 0], preferred_element_type=jnp.float32
            )
            lift_value = jnp.dot(
                everyone, expert_gate_up[e, 1], preferred_element_type=jnp.float32
            )
            hidden_rows = (jax.nn.silu(gate_value) * lift_value).astype(jnp.bfloat16)
            result = jnp.dot(hidden_rows, expert_down[e], preferred_element_type=jnp.float32)
            term = term + own_gates[:, e : e + 1] * result
        routed = lax.psum_scatter(
            term.astype(jnp.bfloat16), "ep", scatter_dimension=0, tiled=True
        ).astype(jnp.float32)
        summed = lax.psum_scatter(
            (shared_part + routed).astype(jnp.bfloat16), "req", scatter_dimension=1, tiled=True
        ).astype(jnp.float32)
        layer_out = (resid_cols.astype(jnp.float32) + summed).astype(jnp.bfloat16)
    starts = cache_len // page_size
    page_now = starts + jnp.mod(req_index - starts, req_count)
    slot_now = jnp.take_along_axis(page_table, page_now[:, None], axis=1)[:, 0]
    old_page = cache_pool[slot_now]
    offsets = (
        page_now[:, None] * page_size
        + jnp.arange(page_size, dtype=jnp.int32)[None, :]
        - cache_len[:, None]
    ).astype(jnp.float32)
    accepted = jnp.take_along_axis(ancestry, accept_leaf[:, None, None], axis=1)[:, 0, :]
    select = accepted[:, None, :] * (depths[:, None, :] == offsets[:, :, None]).astype(jnp.float32)
    written = jnp.einsum(
        "rod,rdk->rok", select.astype(jnp.bfloat16), own_latent, preferred_element_type=jnp.float32
    )
    touched = jnp.sum(select, axis=2) > 0.5
    fresh = jnp.where(touched[..., None], written, old_page.astype(jnp.float32)).astype(
        jnp.bfloat16
    )
    return (layer_out, fresh[:, None])


def solution(mesh):
    in_specs = (
        P("ep", None, None),
        P("ep", None),
        P("ep", "req"),
        P(("req", "ep"), None, None),
        P("ep", None),
        P("ep"),
        P("ep", None),
        P("ep"),
        P(),
        P(),
        P(None, "req"),
        P(),
        P(),
        P("ep", None),
        P("ep", None, None, "req"),
        P("ep", "req", None),
        P(None, None, "req"),
        P("req", None),
    )
    out_specs = (P("ep", "req"), P("ep", "req", None, None))
    return jax.shard_map(
        per_device, mesh=mesh, in_specs=in_specs, out_specs=out_specs, check_vma=False
    )
```

time: 302 us -> 163 us (0.54)
  waiting for transfers between devices: 125 us -> 0 us
  Pallas kernels: 0 us -> 119 us
  matrix products: 70.2 us -> 5.21 us
  blocking collectives: 40.5 us -> 0 us
  other arithmetic: 15.4 us -> 1.58 us
  between operations: 14.2 us -> 0.88 us
    pallas_call x0 -> x2, Pallas kernels: none -> 119 us  [the longest x1 107 us: exchange(): pl.pallas_call(functools.partial(exchange_kernel, n_req, n_ep), out_shape...]
    reduce_scatter x2 -> x0, waiting for transfers between devices: 66.3 us -> none  [the longest x1 45.8 us: per_device(): lax.psum_scatter(term.astype(jnp.bfloat16), 'ep', scatter_dimension=0, ti...]
    dot_general x13 -> x1, matrix products: 67.8 us -> 2.08 us  [per_device(): jnp.einsum('thd,hdl->htl', queries[:, :, :nope_width], absorb_key, prefer...]
    all_gather x2 -> x0, waiting for transfers between devices: 58.5 us -> none  [the longest x1 33.5 us: per_device(): parts = lax.all_gather(projected, 'req').astype(jnp.float32)]
    all_gather x3 -> x0, blocking collectives: 40.5 us -> none  [the longest x1 15.8 us: per_device(): resid = lax.all_gather(resid_cols, 'req', axis=1, tiled=True)]
    unnamed x38 -> x31, local copies, waits for them, and re-layouts: 8.22 us -> 28.1 us
    reduce_sum x5 -> x0, other arithmetic: 9.01 us -> none  [the longest x2 6.06 us: per_device(): totals = jnp.sum(weight_cache, axis=3) + jnp.sum(weight_draft, axis=3)]
    gather x4 -> x0, local copies, waits for them, and re-layouts: 8.13 us -> none  [the longest x2 6.9 us: per_device(): cache_pool[slot_rows]]
  transfers between devices with their start and end apart: 4 -> 0, of which waited for: 4 -> 0; matrix products, arithmetic and copies ran while one was open for 3% -> 0% of each run, Pallas kernels for 0% -> 0%
where the time goes in v2:
time: 163 us; the launch traced here: 160 us
  Pallas kernels  119 us (73%)
  local copies, waits for them, and re-layouts  33.9 us (21%)
  matrix products  5.21 us (3%)
    pallas_call x1, Pallas kernels, exchange(): pl.pallas_call(functools.partial(exchange_kernel, n_req, n_ep), out_shape...  107 us
    unnamed x31, local copies, waits for them, and re-layouts  28.1 us
    pallas_call x1, Pallas kernels, attend(): pl.pallas_call(functools.partial(attend_kernel, scale, page_count), grid_...  11.5 us

profile of v2, /device:TPU:0, one launch (start us, length us, event | category | flops | bytes accessed | tf_op | source)
XLA Modules:
  0.0 160.4 jit_solution(13809452625720400232)
XLA Ops:
  0.7 0.9 copy.88
  1.6 0.6 gather_fusion
  2.3 1.0 convolution_minimum_fusion.5
  3.3 0.2 convolution_minimum_fusion.4
  3.5 0.2 convolution_minimum_fusion.3
  3.7 0.2 convolution_minimum_fusion.2
  3.9 0.2 convolution_minimum_fusion.1
  4.1 0.3 fusion.22
  4.5 0.7 compare_select_fusion.rest_9_
  5.2 1.1 copy.92
  6.3 4.4 %copy.93.rest_0_.rest_1_.rest_2_.rest_3_.rest_4_.rest_5_.rest_6_.rest_7_ = bf16[16,128,576]{2,1,0:T(8,128)(2,1)} copy(bf16[16,128,576]{1,2,0:T(8,128)(2,1)} %param.21) | data formatting | bytes 4718592 | tf_op args[3]
  10.7 2.1 %convolution_convert_fusion.absorbed = bf16[16,128,512]{2,1,0:T(8,128)(2,1)} fusion(bf16[16,128,512]{2,1,0:T(8,128)(2,1)S(1)} %copy-done, bf16[128,16,192]{0,2,1:T(8,128)(2,1)S(1)} %copy-done.6), kind=kOutput, calls=%fused_computation.4 | convolution fusion | flops 269484032 | bytes 4718592 | tf_op jit(solution)/shard_map/thd,hdl->htl/dot_general | solution.py:493
  12.8 0.3 copy.112
  13.1 1.7 %copy-done.1 = bf16[16,128,576]{2,1,0:T(8,128)(2,1)S(1)} copy-done((bf16[16,128,576]{2,1,0:T(8,128)(2,1)S(1)}, bf16[16,128,576]{2,1,0:T(8,128)(2,1)}, u32[]{:S(2)}) %copy-start.1) | copy-done | bytes 2359320
  14.8 1.6 copy-done.2
  16.4 1.6 copy-done.3
  18.0 11.5 %shard_map.185 = (bf16[4,128,512]{2,1,0:T(8,128)(2,1)S(1)}, f32[128,128]{1,0:T(8,128)S(1)}, f32[128,128]{1,0:T(8,128)S(1)}) custom-call(s32[2,8]{1,0:T(2,128)S(1)} %select_bitcast_fusion.slots, bf16[16,128,512]{2,1,0:T(8,128)(2,1)S(1)} %copy-done.2, bf16[16,128,64]{2,1,0:T(8,128)(2,1)S(1)} %bitcast.40, bf16[16,128,576]{2,1,0:T(8,128)(2,1)S(1)} %copy-done.1, ...), custom_call_target="tpu_custom_call" | custom-call | tf_op jit(solution)/shard_map/pallas_call | solution.py:83
  29.5 0.8 copy-done.4
  30.5 0.6 copy.103
  31.1 8.4 %copy.106.gate_up_hbm = bf16[2,2,2048,352]{3,2,1,0:T(8,128)(2,1)} copy(bf16[2,2,2048,352]{2,3,1,0:T(8,128)(2,1)} %param.32) | data formatting | bytes 11534336 | tf_op args[14]
  39.5 4.7 %copy.107.shared_up_hbm = bf16[2,2048,352]{2,1,0:T(8,128)(2,1)} copy(bf16[2,2048,352]{1,2,0:T(8,128)(2,1)} %param.34) | data formatting | bytes 5767168 | tf_op args[16]
  44.2 1.0 copy.104.router
  45.3 0.7 copy.105.named
  46.0 107.3 %shard_map.186 = bf16[128,512]{1,0:T(8,128)(2,1)} custom-call(bf16[4,128,512]{2,1,0:T(8,128)(2,1)} %copy-done.4, f32[4,8,128]{2,1,0:T(8,128)} %bitcast.43, bf16[128,512]{1,0:T(8,128)(2,1)} %hidden.1, bf16[2048,512]{1,0:T(8,128)(2,1)} %out_proj_hbm.1, f32[1,2048]{1,0:T(1,128)} %bitcast.48, bf16[2048,16]{1,0:T(8,128)(2,1)} %copy.104.router, ...), custom_call_target="tpu_custom_call" | custom-call | tf_op jit(solution)/shard_map/pallas_call | solution.py:394
  153.5 0.2 or_reduce_fusion.1
  153.7 0.6 gather_fusion.2
  154.4 0.1 select_reduce_fusion
  154.6 0.2 or_reduce_fusion
  154.8 0.6 gather_fusion.3
  155.5 2.3 %gather_fusion.1 = bf16[2,128,576]{1,2,0:T(8,128)(2,1)S(1)} fusion(bf16[16,128,576]{1,2,0:T(8,128)(2,1)} %param.21, s32[1024]{0:T(1024)S(1)} %pad_clamp_fusion), kind=kCustom, calls=%fused_computation.1 | custom fusion | bytes 589832 | tf_op jit(solution)/shard_map/gather | solution.py:566
  157.8 1.1 fusion.1
  158.8 1.6 copy.114
  (49 shorter events, 0.8 us)
Async XLA Ops:
  0.6 10.1 %copy-start = (bf16[16,128,512]{2,1,0:T(8,128)(2,1)S(1)}, bf16[16,128,512]{2,1,0:T(8,128)(2,1)}, u32[]{:S(2)}) copy-start(bf16[16,128,512]{2,1,0:T(8,128)(2,1)} %param.26) | copy-start | bytes 6291460
  6.3 4.4 %copy-start.6 = (bf16[128,16,192]{0,2,1:T(8,128)(2,1)S(1)}, bf16[128,16,192]{0,2,1:T(8,128)(2,1)}, u32[]{:S(2)}) copy-start(bf16[128,16,192]{0,2,1:T(8,128)(2,1)} %param.18) | copy-start | bytes 2359300
  10.7 2.1 %slice-start = ((bf16[128,16,192]{0,2,1:T(8,128)(2,1)}), bf16[128,16,64]{0,2,1:T(8,128)(2,1)S(1)}, s32[]{:S(2)}) async-start(bf16[128,16,192]{0,2,1:T(8,128)(2,1)} %param.18), calls=%async_computation | async-start | bytes 524288 | tf_op jit(solution)/shard_map/slice | solution.py:496
  13.1 1.7 %copy-start.1 = (bf16[16,128,576]{2,1,0:T(8,128)(2,1)S(1)}, bf16[16,128,576]{2,1,0:T(8,128)(2,1)}, u32[]{:S(2)}) copy-start(bf16[16,128,576]{2,1,0:T(8,128)(2,1)} %copy.93.rest_0_.rest_1_.rest_2_.rest_3_.rest_4_.rest_5_.rest_6_.rest_7_) | copy-start | bytes 7077892
  14.8 1.6 copy-start.2
  16.4 1.6 copy-start.3
  29.5 0.8 copy-start.4
  39.5 4.7 %copy-start.7 = (bf16[2048,16]{0,1:T(8,128)(2,1)S(1)}, bf16[2048,16]{0,1:T(8,128)(2,1)}, u32[]{:S(2)}) copy-start(bf16[2048,16]{0,1:T(8,128)(2,1)} %param.30) | copy-start | bytes 196612
  39.5 5.7 %copy-start.9 = (s32[128,6]{0,1:T(8,128)S(1)}, s32[128,6]{0,1:T(8,128)}, u32[]{:S(2)}) copy-start(s32[128,6]{0,1:T(8,128)} %param.31) | copy-start | bytes 9220
  46.0 107.3 %copy-start.8 = (s32[2]{0:T(128)S(1)}, s32[2]{0:T(128)}, u32[]{:S(2)}) copy-start(s32[2]{0:T(128)} %param.23) | copy-start | bytes 28
  46.0 107.4 %copy-start.10 = (s32[2]{0:T(128)S(1)}, s32[2]{0:T(128)}, u32[]{:S(2)}) copy-start(s32[2]{0:T(128)} %param.25) | copy-start | bytes 28
  46.0 108.8 %copy-start.5 = (s32[2,32]{1,0:T(2,128)S(1)}, s32[2,32]{1,0:T(2,128)}, u32[]{:S(2)}) copy-start(s32[2,32]{1,0:T(2,128)} %param.22) | copy-start | bytes 772

commit v3 on v2

--- a/solution.py
+++ b/solution.py
@@ -13,25 +13,24 @@
 MESH = pl.DeviceIdType.MESH
 
 
-DRAFT_PAD = 128
-
-
 def attend_kernel(scale, page_count, slots, absorbed, rotary, *rest):
     pages = rest[:page_count]
-    drafts, cache_bias, tree_bias, value, projected, peaks, sums, keys, bias = rest[page_count:]
-    page_size = pages[0].shape[1]
+    old_page, drafts, cache_bias, tree_bias, value, select, touched = rest[page_count:-6]
+    projected, peaks, sums, fresh, keys, bias = rest[-6:]
+    page_size = pages[0].shape[2]
     cached = page_count * page_size
-    draft_count = drafts.shape[1]
+    draft_count = tree_bias.shape[1]
     latent_width = absorbed.shape[2]
     head_count = absorbed.shape[0]
     group = head_count // projected.shape[0]
     value_width = value.shape[2]
     for p in range(page_count):
-        keys[p * page_size : (p + 1) * page_size, :] = pages[p][0]
-    keys[cached : cached + draft_count, :] = drafts[0]
-    keys[cached + draft_count :, :] = jnp.zeros(
-        (DRAFT_PAD - draft_count, keys.shape[1]), keys.dtype
-    )
+        keys[:, p * page_size : (p + 1) * page_size] = pages[p][0]
+    keys[:, cached:] = drafts[...]
+    written = jnp.dot(drafts[...], select[0], preferred_element_type=jnp.float32)
+    fresh[0] = jnp.where(
+        touched[0] > 0.5, written, old_page[0].astype(jnp.float32)
+    ).astype(jnp.bfloat16)
     bias[:, :cached] = jnp.broadcast_to(cache_bias[0], (draft_count, cached))
     bias[:, cached:] = tree_bias[0]
     contract_last = (((1,), (1,)), ((), ()))
@@ -42,18 +41,16 @@
         rows = slice(chunk * group, (chunk + 1) * group)
         nope = absorbed[rows].reshape(group * draft_count, latent_width)
         rope = rotary[rows].reshape(group * draft_count, rotary.shape[2])
-        scores = lax.dot_general(
-            nope, keys[:, :latent_width], contract_last, preferred_element_type=jnp.float32
-        ) + lax.dot_general(
-            rope, keys[:, latent_width:], contract_last, preferred_element_type=jnp.float32
-        )
+        scores = jnp.dot(
+            nope, keys[:latent_width, :], preferred_element_type=jnp.float32
+        ) + jnp.dot(rope, keys[latent_width:, :], preferred_element_type=jnp.float32)
         scores = scores.reshape(group, draft_count, -1) * scale + bias[...][None]
         scores = scores.reshape(group * draft_count, -1)
         peak = jnp.maximum(jnp.max(scores, axis=1, keepdims=True), FLOOR)
         weights = jnp.exp(scores - peak)
         total = jnp.sum(weights, axis=1, keepdims=True)
-        mixed = jnp.dot(
-            weights.astype(jnp.bfloat16), keys[:, :latent_width],
+        mixed = lax.dot_general(
+            weights.astype(jnp.bfloat16), keys[:latent_width, :], contract_last,
             preferred_element_type=jnp.float32,
         ).astype(jnp.bfloat16)
         for j in range(group):
@@ -66,16 +63,19 @@
             sums[:, h : h + 1] = total[own]
 
 
-def attend(slots, absorbed, rotary, pool, drafts, cache_bias, tree_bias, value, scale, chunks):
-    requests, page_count = slots.shape
+def attend(
+    slots, absorbed, rotary, pool, drafts, cache_bias, tree_bias, value, select, touched, scale,
+    chunks,
+):
+    requests, page_count = slots.shape[0], slots.shape[1] - 1
     heads, tokens, latent_width = absorbed.shape
-    page_size, key_width = pool.shape[1:]
-    draft_count = drafts.shape[1]
+    key_width, page_size = pool.shape[1:]
+    draft_count = tree_bias.shape[1]
     width = heads // chunks * value.shape[2]
     cached = page_count * page_size
 
     def page_spec(p):
-        return pl.BlockSpec((1, page_size, key_width), lambda r, table: (table[r, p], 0, 0))
+        return pl.BlockSpec((1, key_width, page_size), lambda r, table: (table[r, p], 0, 0))
 
     def by_request(shape):
         return pl.BlockSpec((1,) + shape, lambda r, table: (r, 0, 0))
@@ -88,29 +88,36 @@
             in_specs=[
                 pl.BlockSpec((heads, draft_count, latent_width), lambda r, table: (0, r, 0)),
                 pl.BlockSpec((heads, draft_count, rotary.shape[2]), lambda r, table: (0, r, 0)),
-                *[page_spec(p) for p in range(page_count)],
-                by_request((draft_count, key_width)),
+                *[page_spec(p) for p in range(page_count + 1)],
+                pl.BlockSpec(drafts.shape, lambda r, table: (0, 0)),
                 by_request((1, cached)),
-                by_request((draft_count, DRAFT_PAD)),
+                by_request((draft_count, tokens)),
                 pl.BlockSpec(value.shape, lambda r, table: (0, 0, 0)),
+                by_request((tokens, page_size)),
+                by_request((1, page_size)),
             ],
             out_specs=[
                 pl.BlockSpec((chunks, draft_count, width), lambda r, table: (0, r, 0)),
                 pl.BlockSpec((draft_count, 128), lambda r, table: (r, 0)),
                 pl.BlockSpec((draft_count, 128), lambda r, table: (r, 0)),
+                by_request((key_width, page_size)),
             ],
             scratch_shapes=[
-                pltpu.VMEM((cached + DRAFT_PAD, key_width), jnp.bfloat16),
-                pltpu.VMEM((draft_count, cached + DRAFT_PAD), jnp.float32),
+                pltpu.VMEM((key_width, cached + tokens), jnp.bfloat16),
+                pltpu.VMEM((draft_count, cached + tokens), jnp.float32),
             ],
         ),
         out_shape=[
             jax.ShapeDtypeStruct((chunks, tokens, width), jnp.bfloat16),
             jax.ShapeDtypeStruct((tokens, 128), jnp.float32),
             jax.ShapeDtypeStruct((tokens, 128), jnp.float32),
+            jax.ShapeDtypeStruct((requests, key_width, page_size), jnp.bfloat16),
         ],
-        compiler_params=pltpu.CompilerParams(vmem_limit_bytes=40 * 1024 * 1024),
-    )(slots, absorbed, rotary, *[pool] * page_count, drafts, cache_bias, tree_bias, value)
+        compiler_params=pltpu.CompilerParams(vmem_limit_bytes=58 * 1024 * 1024),
+    )(
+        slots, absorbed, rotary, *[pool] * (page_count + 1), drafts, cache_bias, tree_bias, value,
+        select, touched,
+    )
 
 
 def exchange_kernel(
@@ -131,8 +138,13 @@
     tokens, width = hidden.shape
     group = stats.shape[1] // 2
     value_width = width // group
-    expert_total = named.shape[1]
+    expert_total = named.shape[0]
     local_experts = gate_up.shape[0]
+
+    def across(left, right):
+        return lax.dot_general(
+            left, right, (((1,), (1,)), ((), ())), preferred_element_type=f32
+        )
 
     def partner(s):
         there, bit = 0, 1
@@ -166,28 +178,36 @@
     pl.semaphore_signal(barrier, inc=1, device_id=(req, mate), device_id_type=MESH)
     pl.semaphore_wait(barrier, n_req - 1 + chips)
 
-    def along_z(stage, delta, src, dst):
+    halves = [slice(0, tokens // 2), slice(tokens // 2, tokens)]
+
+    def along_z(stage, delta, src, dst, half=0):
         return pltpu.make_async_remote_copy(
             src_ref=src, dst_ref=dst,
-            send_sem=z_send.at[stage, delta], recv_sem=z_recv.at[stage, delta],
+            send_sem=z_send.at[stage, half, delta], recv_sem=z_recv.at[stage, half, delta],
             device_id=((req + delta) % n_req, ep), device_id_type=MESH,
         )
 
-    sent = []
-    for delta in range(1, n_req):
-        to = (req + delta) % n_req
-        sent.append(along_z(0, delta, parts.at[to], part_in.at[delta]))
-        sent.append(along_z(1, delta, stats.at[to], stat_in.at[delta]))
-    for copy in sent:
+    sent_stats = [
+        along_z(1, d, stats.at[(req + d) % n_req], stat_in.at[d]) for d in range(1, n_req)
+    ]
+    sent_parts = [
+        [
+            along_z(0, d, parts.at[(req + d) % n_req, half], part_in.at[d, half], i)
+            for d in range(1, n_req)
+        ]
+        for i, half in enumerate(halves)
+    ]
+    for copy in sent_stats + sent_parts[0] + sent_parts[1]:
         copy.start()
     part_in[0] = parts[req]
     stat_in[0] = stats[req]
-    for copy in sent:
+    for copy in sent_stats:
         copy.wait()
 
     flat = stat_in[...].reshape(n_req * 2 * group, tokens)
     flat = jnp.concatenate([flat, jnp.zeros((128 - flat.shape[0], tokens), f32)], axis=0)
     columns = flat.T
+    factors = []
     for j in range(group):
         at = [d * 2 * group + j for d in range(n_req)]
         peak = [columns[:, i : i + 1] for i in at]
@@ -195,34 +215,51 @@
         top = functools.reduce(jnp.maximum, peak)
         factor = [jnp.exp(p - top) for p in peak]
         inverse = 1.0 / sum(f * t for f, t in zip(factor, total_at))
-        lanes = slice(j * value_width, (j + 1) * value_width)
-        head = sum(
-            part_in[d, :, lanes].astype(f32) * (factor[d] * inverse) for d in range(n_req)
-        )
-        head_in[0, :, lanes] = head.astype(bf16)
-
-    sent = [along_z(2, d, head_in.at[0], head_in.at[d]) for d in range(1, n_req)]
-    for copy in sent:
-        copy.start()
+        factors.append([f * inverse for f in factor])
+
+    sent_heads = []
+    for i, half in enumerate(halves):
+        for copy in sent_parts[i]:
+            copy.wait()
+        for j in range(group):
+            lanes = slice(j * value_width, (j + 1) * value_width)
+            head = sum(
+                part_in[d, half, lanes].astype(f32) * factors[j][d][half] for d in range(n_req)
+            )
+            head_in[0, half, lanes] = head.astype(bf16)
+        sent_heads.append(
+            [
+                along_z(2, d, head_in.at[0, half], head_in.at[d, half], i)
+                for d in range(1, n_req)
+            ]
+        )
+        for copy in sent_heads[i]:
+            copy.start()
     loads[0].wait()
 
-    def project(delta):
+    def project(delta, half):
         src = (req + n_req - delta) % n_req
         return jnp.dot(
-            head_in[delta], out_proj[pl.ds(pl.multiple_of(src * width, width), width), :],
+            head_in[delta, half], out_proj[pl.ds(pl.multiple_of(src * width, width), width), :],
             preferred_element_type=f32,
         )
 
-    attention = project(0)
-    for d in range(1, n_req):
-        sent[d - 1].wait()
-        attention = attention + project(d)
-    own_resid = (hidden[...].astype(f32) + attention).astype(bf16)
-    resid_in[req] = own_resid
-    sent = [along_z(3, d, resid_in.at[req], resid_in.at[req]) for d in range(1, n_req)]
-    for copy in sent:
-        copy.start()
-    for copy in sent:
+    sent_resid = []
+    for i, half in enumerate(halves):
+        attention = project(0, half)
+        for d in range(1, n_req):
+            sent_heads[i][d - 1].wait()
+            attention = attention + project(d, half)
+        resid_in[req, half] = (hidden[half].astype(f32) + attention).astype(bf16)
+        sent_resid.append(
+            [
+                along_z(3, d, resid_in.at[req, half], resid_in.at[req, half], i)
+                for d in range(1, n_req)
+            ]
+        )
+        for copy in sent_resid[i]:
+            copy.start()
+    for copy in sent_resid[0] + sent_resid[1]:
         copy.wait()
 
     square = 0.0
@@ -235,11 +272,9 @@
         rows[0, 0, :, lanes] = (
             resid_in[d].astype(f32) * inverse * gain[:, lanes]
         ).astype(bf16)
-    logits = jnp.dot(rows[0, 0], router[...], preferred_element_type=f32)
+    logits = across(router[...], rows[0, 0])
     lifted = named[...] / (1.0 + jnp.exp(-logits))
-    gate = lifted / jnp.sum(lifted, axis=1, keepdims=True)
-    gate = jnp.concatenate([gate, jnp.zeros((tokens, 128 - expert_total), f32)], axis=1)
-    gates[0, 0] = gate.T[:expert_total]
+    gates[0, 0] = lifted / jnp.sum(lifted, axis=0, keepdims=True)
 
     def spread(s):
         to = (req, partner(s))
@@ -276,7 +311,8 @@
             device_id=(req, partner(s)), device_id_type=MESH,
         )
 
-    for s in range(1, chips):
+    last_after_first = chips > 2
+    for s in range(1, chips - 1 if last_after_first else chips):
         for copy in spread(s):
             copy.start()
     for copy in forward(0):
@@ -288,8 +324,8 @@
     loads[1].wait()
     loads[2].wait()
     shared_hidden = silu_times(
-        jnp.dot(rows[0, 0], shared_up[0], preferred_element_type=f32),
-        jnp.dot(rows[0, 0], shared_up[1], preferred_element_type=f32),
+        across(rows[0, 0], shared_up[0]),
+        across(rows[0, 0], shared_up[1]),
     ).astype(bf16)
     total[...] = jnp.dot(shared_hidden, shared_down[...], preferred_element_type=f32)
     loads[3].wait()
@@ -302,6 +338,12 @@
                 copy.wait_recv()
             for copy in forward(s):
                 copy.start()
+
+        if last_after_first:
+            @pl.when(s == 1)
+            def _():
+                for copy in spread(chips - 1):
+                    copy.start()
 
         for copy in forward(s):
             copy.wait_recv()
@@ -319,8 +361,8 @@
                 jnp.where(lane == ep * local_experts + e, own_gate, 0.0), axis=1, keepdims=True
             )
             hidden_rows = silu_times(
-                jnp.dot(both, gate_up[e, 0], preferred_element_type=f32),
-                jnp.dot(both, gate_up[e, 1], preferred_element_type=f32),
+                across(both, gate_up[e, 0]),
+                across(both, gate_up[e, 1]),
             )
             weighted.append((hidden_rows * column).astype(bf16))
 
@@ -405,10 +447,10 @@
             pltpu.VMEM((n_req, tokens, width), bf16),
             pltpu.VMEM((n_req, tokens, width), bf16),
             pltpu.VMEM((n_req, tokens, width), bf16),
-            dma((5, n_req)),
-            dma((5, n_req)),
+            dma((5, 2, n_req)),
+            dma((5, 2, n_req)),
             pltpu.VMEM((chips, 2, tokens, model), bf16),
-            pltpu.VMEM((chips, 2, named.shape[1], tokens), f32),
+            pltpu.VMEM((chips, 2, named.shape[0], tokens), f32),
             pltpu.VMEM((chips, tokens, model), bf16),
             pltpu.VMEM((chips, tokens, model), bf16),
             pltpu.VMEM((chips, tokens, model), bf16),
@@ -470,14 +512,23 @@
     nope_width = absorb_key.shape[1]
     latent_width = absorb_key.shape[2]
     page_size = cache_pool.shape[1]
-    key_width = cache_pool.shape[2]
     page_count = page_table.shape[1]
     score_scale = 1.0 / math.sqrt(queries.shape[2])
     ancestry = ancestors(parents)
     depths = jnp.sum(ancestry, axis=2) - 1.0
     local_pages = page_count // req_count
     page_cols = req_index + req_count * jnp.arange(local_pages, dtype=jnp.int32)
-    slot_rows = jnp.take(page_table, page_cols, axis=1)
+    own_column = jnp.arange(req_count, dtype=jnp.int32) == req_index
+    slot_rows = jnp.sum(
+        jnp.where(own_column, page_table.reshape(request_count, local_pages, req_count), 0), axis=2
+    )
+    starts = cache_len // page_size
+    page_now = starts + jnp.mod(req_index - starts, req_count)
+    all_pages = jnp.arange(page_count, dtype=jnp.int32)
+    slot_now = jnp.sum(
+        jnp.where(all_pages[None, :] == page_now[:, None], page_table, 0), axis=1, keepdims=True
+    )
+    slots = jnp.concatenate([slot_rows, slot_now], axis=1)
     positions = (
         page_cols[:, None] * page_size + jnp.arange(page_size, dtype=jnp.int32)[None, :]
     ).reshape(-1)
@@ -486,17 +537,28 @@
     draft_index = jnp.arange(draft_count, dtype=jnp.int32)
     own_draft = draft_index // draft_share == req_index
     tree_bias = jnp.where((ancestry > 0.5) & own_draft[None, None, :], 0.0, NEGATIVE)
-    tree_bias = jnp.pad(
-        tree_bias, ((0, 0), (0, 0), (0, DRAFT_PAD - draft_count)), constant_values=NEGATIVE
-    )
-    own_latent = draft_latent.reshape(request_count, draft_count, key_width)
+    same_request = jnp.eye(request_count, dtype=jnp.float32)
+    tree_bias = jnp.where(
+        same_request[:, None, :, None] > 0.5, tree_bias[:, :, None, :], NEGATIVE
+    ).reshape(request_count, draft_count, token_count)
+    offsets = (
+        page_now[:, None] * page_size
+        + jnp.arange(page_size, dtype=jnp.int32)[None, :]
+        - cache_len[:, None]
+    ).astype(jnp.float32)
+    is_leaf = (draft_index[None, :] == accept_leaf[:, None]).astype(jnp.float32)
+    accepted = jnp.sum(ancestry * is_leaf[:, :, None], axis=1)
+    select = accepted[:, :, None] * (depths[:, :, None] == offsets[:, None, :]).astype(jnp.float32)
+    touched = jnp.sum(select, axis=1, keepdims=True)
+    select = (same_request[:, :, None, None] * select[:, None]).astype(jnp.bfloat16)
+    select = select.reshape(request_count, token_count, page_size)
     absorbed = jnp.einsum(
         "thd,hdl->htl", queries[:, :, :nope_width], absorb_key, preferred_element_type=jnp.float32
     ).astype(jnp.bfloat16)
     rotary = jnp.transpose(queries[:, :, nope_width:], (1, 0, 2))
-    projected, peaks, sums = attend(
-        slot_rows, absorbed, rotary, cache_pool, own_latent, cache_bias, tree_bias, absorb_value,
-        score_scale, req_count,
+    projected, peaks, sums, fresh = attend(
+        slots, absorbed, rotary, jnp.swapaxes(cache_pool, 1, 2), draft_latent.T, cache_bias,
+        tree_bias, absorb_value, select, touched, score_scale, req_count,
     )
     local_experts = expert_gate_up.shape[0]
     expert_total = local_experts * ep_count
@@ -509,8 +571,9 @@
         by_head = by_head.reshape(2, req_count, group, token_count)
         by_head = jnp.transpose(by_head, (1, 0, 2, 3)).reshape(req_count, 2 * group, token_count)
         layer_out = exchange(
-            projected, by_head, hidden_in, out_proj, norm_gain.reshape(1, -1), router, named,
-            expert_gate_up, expert_down, shared_gate_up, shared_down, req_count, ep_count,
+            projected, by_head, hidden_in, out_proj, norm_gain.reshape(1, -1), router.T, named.T,
+            jnp.swapaxes(expert_gate_up, 2, 3), expert_down, jnp.swapaxes(shared_gate_up, 1, 2),
+            shared_down, req_count, ep_count,
         )
     else:
         stats = lax.all_gather(jnp.stack([peaks, sums]), "req")
@@ -560,25 +623,7 @@
             (shared_part + routed).astype(jnp.bfloat16), "req", scatter_dimension=1, tiled=True
         ).astype(jnp.float32)
         layer_out = (resid_cols.astype(jnp.float32) + summed).astype(jnp.bfloat16)
-    starts = cache_len // page_size
-    page_now = starts + jnp.mod(req_index - starts, req_count)
-    slot_now = jnp.take_along_axis(page_table, page_now[:, None], axis=1)[:, 0]
-    old_page = cache_pool[slot_now]
-    offsets = (
-        page_now[:, None] * page_size
-        + jnp.arange(page_size, dtype=jnp.int32)[None, :]
-        - cache_len[:, None]
-    ).astype(jnp.float32)
-    accepted = jnp.take_along_axis(ancestry, accept_leaf[:, None, None], axis=1)[:, 0, :]
-    select = accepted[:, None, :] * (depths[:, None, :] == offsets[:, :, None]).astype(jnp.float32)
-    written = jnp.einsum(
-        "rod,rdk->rok", select.astype(jnp.bfloat16), own_latent, preferred_element_type=jnp.float32
-    )
-    touched = jnp.sum(select, axis=2) > 0.5
-    fresh = jnp.where(touched[..., None], written, old_page.astype(jnp.float32)).astype(
-        jnp.bfloat16
-    )
-    return (layer_out, fresh[:, None])
+    return (layer_out, jnp.swapaxes(fresh, 1, 2)[:, None])
 
 
 def solution(mesh):

time: 163 us -> 138 us (0.85); the launches traced: 160 us -> 138 us
  local copies, waits for them, and re-layouts: 33.9 us -> 5.61 us
  other arithmetic: 1.58 us -> 7.85 us
    unnamed x31 -> x8, local copies, waits for them, and re-layouts: 28.1 us -> 2.62 us
    gather x7 -> x0, local copies, waits for them, and re-layouts: 4.31 us -> none  [the longest x1 2.27 us: per_device(): old_page = cache_pool[slot_now]]
    pallas_call x1, Pallas kernels: 11.5 us -> 14.8 us  [attend(): pl.pallas_call(functools.partial(attend_kernel, scale, page_count), grid_...]
    pallas_call x1, Pallas kernels: 107 us -> 105 us  [exchange(): pl.pallas_call(functools.partial(exchange_kernel, n_req, n_ep), out_shape...]
where the time goes in v3:
time: 138 us
  Pallas kernels  119 us (86%)
  other arithmetic  7.85 us (6%)
  local copies, waits for them, and re-layouts  5.61 us (4%)
  matrix products  4.29 us (3%)
    pallas_call x1, Pallas kernels, exchange(): pl.pallas_call(functools.partial(exchange_kernel, n_req, n_ep), out_shape...  105 us
    pallas_call x1, Pallas kernels, attend(): pl.pallas_call(functools.partial(attend_kernel, scale, page_count), grid_...  14.8 us

profile of v3, /device:TPU:0, one launch (start us, length us, event | category | flops | bytes accessed | tf_op | source)
XLA Modules:
  0.0 137.9 jit_solution(11165543295868279851)
XLA Ops:
  0.7 1.1 convolution_minimum_fusion.5
  1.8 0.2 convolution_minimum_fusion.4
  2.0 0.2 convolution_minimum_fusion.3
  2.2 0.2 convolution_minimum_fusion.2
  2.4 0.2 convolution_minimum_fusion.1
  2.6 0.7 compare_convert_fusion
  3.3 0.3 fusion.13
  3.7 0.7 broadcast_multiply_fusion
  4.3 0.7 subtract_convert_fusion
  5.1 0.7 fusion.8
  5.7 0.1 mul.57
  5.8 0.1 mul.58
  5.9 0.7 fusion.1.rest_13_
  6.6 0.9 fusion.9
  7.5 0.1 copy.35
  7.6 0.8 reshape.188
  8.3 0.1 select_reduce_fusion
  8.5 0.6 pad_add_fusion.slots
  9.2 0.1 broadcast_in_dim.100
  9.3 0.1 broadcast_in_dim.94
  9.4 0.1 broadcast_in_dim.95
  9.5 0.6 broadcast_select_fusion.rest_11_
  10.1 0.1 add_bitcast_fusion
  10.2 1.3 compare_select_fusion.1.rest_10_
  11.5 2.1 %convolution_convert_fusion.absorbed = bf16[16,128,512]{2,1,0:T(8,128)(2,1)} fusion(bf16[16,128,512]{2,1,0:T(8,128)(2,1)S(1)} %copy-done, bf16[128,16,192]{0,2,1:T(8,128)(2,1)S(1)} %copy-done.1), kind=kOutput, calls=%fused_computation | convolution fusion | flops 269484032 | bytes 4718592 | tf_op jit(solution)/shard_map/thd,hdl->htl/dot_general | solution.py:555
  13.6 1.0 copy.43
  14.7 14.8 %shard_map.185 = (bf16[4,128,512]{2,1,0:T(8,128)(2,1)}, f32[128,128]{1,0:T(8,128)}, f32[128,128]{1,0:T(8,128)}, bf16[2,576,128]{2,1,0:T(8,128)(2,1)}) custom-call(s32[2,9]{1,0:T(2,128)} %pad_add_fusion.slots, bf16[16,128,512]{2,1,0:T(8,128)(2,1)} %convolution_convert_fusion.absorbed, bf16[16,128,64]{2,1,0:T(8,128)(2,1)} %bitcast.53, ...), custom_call_target="tpu_custom_call" | custom-call | tf_op jit(solution)/shard_map/pallas_call | solution.py:83
  29.5 0.9 slice_bitcast_fusion
  30.5 0.6 copy.40
  31.2 0.6 convert_bitcast_fusion.named
  31.8 104.5 %shard_map.186 = bf16[128,512]{1,0:T(8,128)(2,1)} custom-call(bf16[4,128,512]{2,1,0:T(8,128)(2,1)} %get-tuple-element.6.parts, f32[4,8,128]{2,1,0:T(8,128)} %bitcast.56, bf16[128,512]{1,0:T(8,128)(2,1)} %hidden.1, bf16[2048,512]{1,0:T(8,128)(2,1)} %out_proj_hbm.1, f32[1,2048]{1,0:T(1,128)} %bitcast.59, bf16[16,2048]{1,0:T(8,128)(2,1)} %bitcast.55, ...), custom_call_target="tpu_custom_call" | custom-call | tf_op jit(solution)/shard_map/pallas_call | solution.py:436
  136.3 1.6 %copy.45 = bf16[128,512]{1,0:T(8,128)(2,1)} copy(bf16[128,512]{1,0:T(8,128)(2,1)} %shard_map.186) | data formatting | bytes 262144
  (20 shorter events, 0.2 us)
Async XLA Ops:
  0.6 10.9 %copy-start = (bf16[16,128,512]{2,1,0:T(8,128)(2,1)S(1)}, bf16[16,128,512]{2,1,0:T(8,128)(2,1)}, u32[]{:S(2)}) copy-start(bf16[16,128,512]{2,1,0:T(8,128)(2,1)} %param.26) | copy-start | bytes 6291460
  0.6 10.9 %copy-start.1 = (bf16[128,16,192]{0,2,1:T(8,128)(2,1)S(1)}, bf16[128,16,192]{0,2,1:T(8,128)(2,1)}, u32[]{:S(2)}) copy-start(bf16[128,16,192]{0,2,1:T(8,128)(2,1)} %param.18) | copy-start | bytes 2359300
  11.5 2.1 %slice-start = ((bf16[128,16,192]{0,2,1:T(8,128)(2,1)}), bf16[128,16,64]{0,2,1:T(8,128)(2,1)S(1)}, s32[]{:S(2)}) async-start(bf16[128,16,192]{0,2,1:T(8,128)(2,1)} %param.18), calls=%async_computation | async-start | bytes 524288 | tf_op jit(solution)/shard_map/slice | solution.py:558
  14.7 16.5 %copy-start.2 = (s32[128,6]{0,1:T(8,128)S(1)}, s32[128,6]{0,1:T(8,128)}, u32[]{:S(2)}) copy-start(s32[128,6]{0,1:T(8,128)} %param.31) | copy-start | bytes 9220

commit v4 on v3

--- a/solution.py
+++ b/solution.py
@@ -332,18 +332,27 @@
     loads[4].wait()
 
     def step(s, carry):
-        @pl.when(s > 0)
+        if last_after_first:
+            @pl.when(s == 1)
+            def _():
+                for copy in spread(1):
+                    copy.wait_recv()
+                for copy in forward(1):
+                    copy.start()
+                for copy in spread(chips - 1):
+                    copy.start()
+                for early in range(2, chips - 1):
+                    for copy in spread(early):
+                        copy.wait_recv()
+                    for copy in forward(early):
+                        copy.start()
+
+        @pl.when(s == chips - 1 if last_after_first else s > 0)
         def _():
             for copy in spread(s):
                 copy.wait_recv()
             for copy in forward(s):
                 copy.start()
-
-        if last_after_first:
-            @pl.when(s == 1)
-            def _():
-                for copy in spread(chips - 1):
-                    copy.start()
 
         for copy in forward(s):
             copy.wait_recv()

time: 138 us -> 138 us (level)
  no operation moved by 1% of the time
where the time goes in v4:
time: 138 us
  Pallas kernels  119 us (86%)
  other arithmetic  7.85 us (6%)
  local copies, waits for them, and re-layouts  5.61 us (4%)
  matrix products  4.29 us (3%)
    pallas_call x1, Pallas kernels, exchange(): pl.pallas_call(functools.partial(exchange_kernel, n_req, n_ep), out_shape...  104 us
    pallas_call x1, Pallas kernels, attend(): pl.pallas_call(functools.partial(attend_kernel, scale, page_count), grid_...  14.8 us

profile of v4, /device:TPU:0, one launch (start us, length us, event | category | flops | bytes accessed | tf_op | source)
XLA Modules:
  0.0 137.8 jit_solution(5905471565257338211)
XLA Ops:
  0.7 1.1 convolution_minimum_fusion.5
  1.8 0.2 convolution_minimum_fusion.4
  2.0 0.2 convolution_minimum_fusion.3
  2.2 0.2 convolution_minimum_fusion.2
  2.4 0.2 convolution_minimum_fusion.1
  2.6 0.7 compare_convert_fusion
  3.3 0.3 fusion.13
  3.7 0.7 broadcast_multiply_fusion
  4.3 0.7 subtract_convert_fusion
  5.1 0.7 fusion.8
  5.7 0.1 mul.57
  5.8 0.1 mul.58
  5.9 0.7 fusion.1.rest_13_
  6.6 0.9 fusion.9
  7.5 0.1 copy.35
  7.6 0.8 reshape.188
  8.3 0.1 select_reduce_fusion
  8.5 0.6 pad_add_fusion.slots
  9.2 0.1 broadcast_in_dim.100
  9.3 0.1 broadcast_in_dim.94
  9.4 0.1 broadcast_in_dim.95
  9.5 0.6 broadcast_select_fusion.rest_11_
  10.1 0.1 add_bitcast_fusion
  10.2 1.3 compare_select_fusion.1.rest_10_
  11.5 2.1 %convolution_convert_fusion.absorbed = bf16[16,128,512]{2,1,0:T(8,128)(2,1)} fusion(bf16[16,128,512]{2,1,0:T(8,128)(2,1)S(1)} %copy-done, bf16[128,16,192]{0,2,1:T(8,128)(2,1)S(1)} %copy-done.1), kind=kOutput, calls=%fused_computation | convolution fusion | flops 269484032 | bytes 4718592 | tf_op jit(solution)/shard_map/thd,hdl->htl/dot_general | solution.py:564
  13.6 1.0 copy.43
  14.7 14.8 %shard_map.185 = (bf16[4,128,512]{2,1,0:T(8,128)(2,1)}, f32[128,128]{1,0:T(8,128)}, f32[128,128]{1,0:T(8,128)}, bf16[2,576,128]{2,1,0:T(8,128)(2,1)}) custom-call(s32[2,9]{1,0:T(2,128)} %pad_add_fusion.slots, bf16[16,128,512]{2,1,0:T(8,128)(2,1)} %convolution_convert_fusion.absorbed, bf16[16,128,64]{2,1,0:T(8,128)(2,1)} %bitcast.53, ...), custom_call_target="tpu_custom_call" | custom-call | tf_op jit(solution)/shard_map/pallas_call | solution.py:83
  29.5 0.9 slice_bitcast_fusion
  30.5 0.6 copy.40
  31.2 0.6 convert_bitcast_fusion.named
  31.8 104.4 %shard_map.186 = bf16[128,512]{1,0:T(8,128)(2,1)} custom-call(bf16[4,128,512]{2,1,0:T(8,128)(2,1)} %get-tuple-element.6.parts, f32[4,8,128]{2,1,0:T(8,128)} %bitcast.56, bf16[128,512]{1,0:T(8,128)(2,1)} %hidden.1, bf16[2048,512]{1,0:T(8,128)(2,1)} %out_proj_hbm.1, f32[1,2048]{1,0:T(1,128)} %bitcast.59, bf16[16,2048]{1,0:T(8,128)(2,1)} %bitcast.55, ...), custom_call_target="tpu_custom_call" | custom-call | tf_op jit(solution)/shard_map/pallas_call | solution.py:445
  136.2 1.6 %copy.45 = bf16[128,512]{1,0:T(8,128)(2,1)} copy(bf16[128,512]{1,0:T(8,128)(2,1)} %shard_map.186) | data formatting | bytes 262144
  (20 shorter events, 0.2 us)
Async XLA Ops:
  0.6 10.9 %copy-start = (bf16[16,128,512]{2,1,0:T(8,128)(2,1)S(1)}, bf16[16,128,512]{2,1,0:T(8,128)(2,1)}, u32[]{:S(2)}) copy-start(bf16[16,128,512]{2,1,0:T(8,128)(2,1)} %param.26) | copy-start | bytes 6291460
  0.6 10.9 %copy-start.1 = (bf16[128,16,192]{0,2,1:T(8,128)(2,1)S(1)}, bf16[128,16,192]{0,2,1:T(8,128)(2,1)}, u32[]{:S(2)}) copy-start(bf16[128,16,192]{0,2,1:T(8,128)(2,1)} %param.18) | copy-start | bytes 2359300
  11.5 2.1 %slice-start = ((bf16[128,16,192]{0,2,1:T(8,128)(2,1)}), bf16[128,16,64]{0,2,1:T(8,128)(2,1)S(1)}, s32[]{:S(2)}) async-start(bf16[128,16,192]{0,2,1:T(8,128)(2,1)} %param.18), calls=%async_computation | async-start | bytes 524288 | tf_op jit(solution)/shard_map/slice | solution.py:567
  14.7 16.5 %copy-start.2 = (s32[128,6]{0,1:T(8,128)S(1)}, s32[128,6]{0,1:T(8,128)}, u32[]{:S(2)}) copy-start(s32[128,6]{0,1:T(8,128)} %param.31) | copy-start | bytes 9220
